TPU v7x, 512 devices: a whole 4x8x8 slice. The times are simulated.
512 devices in a mesh: shot: 16 (over z, core), gx: 8 (over y), gy: 4 (over x).
Axes of the slice: x: 4, y: 8, z: 8, core: 2. Of those that a mesh axis runs over, the one named last changes fastest.
Arguments:
- fields_now: float32 [16, 4, 8, 512, 512], P('shot', None, None, 'gx', 'gy'), may hold values from -6 to 6
- fields_before: float32 [16, 4, 8, 512, 512], P('shot', None, None, 'gx', 'gy'), may hold values from -6 to 6
- speed_sq: float32 [8, 512, 512], P(None, 'gx', 'gy'), may hold values from 0.04 to 0.16
- born_dir: float32 [8, 512, 512], P(None, 'gx', 'gy'), may hold values from -1.5 to 1.5
- pml_x: int32 [512], replicated, may hold values from 0 to 16, as said below
- pml_y: int32 [512], replicated, may hold values from 0 to 16, as said below
- src_x: int32 [16], P('shot'), may hold values from 0 to 511
- src_y: int32 [16], P('shot'), may hold values from 0 to 511
- src_amp: float32 [16, 2], P('shot'), may hold values from -8 to 8
- rec_x: int32 [16, 512], P('shot'), may hold values from 0 to 511
- rec_y: int32 [16, 512], P('shot'), may hold values from 0 to 511
- residual: float32 [16, 2, 512], P('shot'), may hold values from -6 to 6
Outputs:
- fields_after: float32 [16, 4, 8, 512, 512], P('shot', None, None, 'gx', 'gy')
- gradient: float32 [8, 512, 512], P(None, 'gx', 'gy')
- hess_vec: float32 [8, 512, 512], P(None, 'gx', 'gy')
- curvature: float32 [], replicated
Inputs may be any that keep to these rules, and one draw needn't show every extreme that they name: pml_x[i] is the larger of max(0, 16 - i) and max(0, w - (511 - i)), with w between 8 and 16 drawn once. pml_y[i] is the larger of max(0, 16 - i) and max(0, w - (511 - i)), with w between 8 and 16 drawn once.
All inputs are finite; a program needn't handle non-finite values.
Results may differ from a plain program's by a relative error of at most 0.00045.
Values sent between devices are 32-bit elements; how exact they have to be, the bound alone decides.
A program may use at most 64 MiB of HBM per device.

v0:
```python
import math

import jax
import jax.numpy as jnp
from jax import lax
from jax.sharding import PartitionSpec as P

PML_W = 16


COEFS = (-205.0 / 72.0, 8.0 / 5.0, -1.0 / 5.0, 8.0 / 315.0, -1.0 / 560.0)
DAMP = 1.0


def with_halo(cells, sides, width):
    for axis, dim in sides:
        count = lax.axis_size(axis)
        ends = count - 1
        head = lax.slice_in_dim(cells, 0, width, axis=dim)
        tail = lax.slice_in_dim(cells, cells.shape[dim] - width, cells.shape[dim], axis=dim)
        cells = jnp.concatenate(
            [
                lax.ppermute(tail, axis, [(i, (i + 1) % count) for i in range(ends)]),
                cells,
                lax.ppermute(head, axis, [((i + 1) % count, i) for i in range(ends)]),
            ],
            axis=dim,
        )
    return cells


def laplace(wavefield):
    levels = wavefield.shape[-3]
    row_count = wavefield.shape[-2] - 8
    column_count = wavefield.shape[-1] - 8
    padding = [(0, 0)] * (wavefield.ndim - 3) + [(4, 4), (0, 0), (0, 0)]
    padded = jnp.pad(wavefield, padding)
    summed = 3.0 * COEFS[0] * wavefield[..., 4 : 4 + row_count, 4 : 4 + column_count]
    for offset in range(1, 5):
        neighbours = (
            wavefield[..., 4 + offset : 4 + offset + row_count, 4 : 4 + column_count]
            + wavefield[..., 4 - offset : 4 - offset + row_count, 4 : 4 + column_count]
            + wavefield[..., 4 : 4 + row_count, 4 + offset : 4 + offset + column_count]
            + wavefield[..., 4 : 4 + row_count, 4 - offset : 4 - offset + column_count]
            + padded[..., 4 + offset : 4 + offset + levels, 4 : 4 + row_count, 4 : 4 + column_count]
            + padded[..., 4 - offset : 4 - offset + levels, 4 : 4 + row_count, 4 : 4 + column_count]
        )
        summed = summed + COEFS[offset] * neighbours
    return summed


def injection(anchor_x, anchor_y, extent_x, extent_y, where_x, where_y, weights):
    cells_x = anchor_x + jnp.arange(extent_x, dtype=jnp.int32)
    cells_y = anchor_y + jnp.arange(extent_y, dtype=jnp.int32)
    left_hot = (where_x[:, None] == cells_x[None, :]).astype(jnp.float32) * weights[:, None]
    right_hot = (where_y[:, None] == cells_y[None, :]).astype(jnp.float32)
    return jnp.einsum("ra,rb->ab", left_hot, right_hot, precision=lax.Precision.HIGHEST)


def damping(pml_x, pml_y, anchor_x, anchor_y, extent_x, extent_y):
    index_x = jnp.clip(anchor_x + jnp.arange(extent_x, dtype=jnp.int32), 0, pml_x.shape[0] - 1)
    index_y = jnp.clip(anchor_y + jnp.arange(extent_y, dtype=jnp.int32), 0, pml_y.shape[0] - 1)
    layer_x = jnp.take(pml_x, index_x).astype(jnp.float32) / PML_W
    layer_y = jnp.take(pml_y, index_y).astype(jnp.float32) / PML_W
    return DAMP * (layer_x[:, None] * layer_x[:, None] + layer_y[None, :] * layer_y[None, :])


def advance(
    current,
    previous,
    lap_now,
    speed_sq,
    born_dir,
    damp,
    source_plane,
    receiver_plane,
    counts,
    level_mask,
):
    drive = jnp.stack(
        [
            level_mask * source_plane,
            born_dir * lap_now[0],
            level_mask * receiver_plane,
            born_dir * lap_now[2] + level_mask * counts * current[1],
        ]
    )
    return (2.0 * current - (1.0 - damp) * previous + speed_sq * lap_now + drive) / (1.0 + damp)


def local(
    fields_now,
    fields_before,
    speed_sq,
    born_dir,
    pml_x,
    pml_y,
    src_x,
    src_y,
    src_amp,
    rec_x,
    rec_y,
    residual,
):
    shot_count = fields_now.shape[0]
    levels, extent_x, extent_y = speed_sq.shape
    corner_x = lax.axis_index("gx") * extent_x
    corner_y = lax.axis_index("gy") * extent_y
    whole_x = extent_x * lax.axis_size("gx")
    whole_y = extent_y * lax.axis_size("gy")
    level_mask = (jnp.arange(levels) == 1).astype(jnp.float32)[:, None, None]
    damp_inner = damping(pml_x, pml_y, corner_x, corner_y, extent_x, extent_y)
    grad_part = jnp.zeros(speed_sq.shape, jnp.float32)
    hess_part = jnp.zeros(speed_sq.shape, jnp.float32)
    ones_rec = jnp.ones(rec_x.shape[1:], jnp.float32)
    current = fields_now[0]
    previous = fields_before[0]
    counts_inner = injection(corner_x, corner_y, extent_x, extent_y, rec_x[0], rec_y[0], ones_rec)
    for turn in range(2):
        padded = with_halo(current, (("gx", 2), ("gy", 3)), 4)
        lap_now = laplace(padded)
        source_plane = injection(
            corner_x, corner_y, extent_x, extent_y, src_x, src_y, src_amp[0, turn : turn + 1]
        )
        receiver_plane = injection(
            corner_x, corner_y, extent_x, extent_y, rec_x[0], rec_y[0], residual[0, turn]
        )
        source_plane, receiver_plane = (source_plane, receiver_plane)
        grad_part = grad_part + current[2] * lap_now[0]
        hess_part = hess_part + current[3] * lap_now[0] + current[2] * lap_now[1]
        stepped = advance(
            current,
            previous,
            lap_now,
            speed_sq,
            born_dir,
            damp_inner,
            source_plane,
            receiver_plane,
            counts_inner,
            level_mask,
        )
        previous = current
        current = stepped
    finals = [current]
    fields_after = jnp.stack(finals)
    shots_total = shot_count * lax.axis_size("shot")
    scale_cells = 1.0 / math.sqrt(levels * whole_x * whole_y)
    grad_sum, hess_sum = lax.psum((grad_part, hess_part), "shot")
    curvature = lax.psum(jnp.sum(born_dir * hess_sum), ("gx", "gy")) / shots_total * scale_cells
    gradient = grad_sum / shots_total
    hess_vec = hess_sum / shots_total
    return (fields_after, gradient, hess_vec, curvature)


def solution(mesh):
    placed = (
        P("shot", None, None, "gx", "gy"),
        P("shot", None, None, "gx", "gy"),
        P(None, "gx", "gy"),
        P(None, "gx", "gy"),
        P(),
        P(),
        P("shot"),
        P("shot"),
        P("shot", None),
        P("shot", None),
        P("shot", None),
        P("shot", None, None),
    )
    return jax.shard_map(
        local,
        mesh=mesh,
        in_specs=placed,
        out_specs=(
            P("shot", None, None, "gx", "gy"),
            P(None, "gx", "gy"),
            P(None, "gx", "gy"),
            P(),
        ),
        check_vma=False,
    )
```

profile of v0, /device:TPU:32, one launch (start us, length us, event | category | flops | bytes accessed | tf_op | source)
XLA Modules:
  0.0 331.4 jit_solution(16576026124243335923)
XLA Ops:
  7.2 0.0 copy-start
  7.2 0.0 all-reduce.5.cloned.1.call-start
  7.3 1.8 copy.69
  9.1 2.4 collective-permute-start
  11.5 3.5 %collective-permute-start.1 = (f32[4,8,4,128]{3,1,2,0:T(8,128)S(1)}, f32[4,8,4,128]{3,1,2,0:T(8,128)S(1)}, u32[]{:S(2)}, u32[]{:S(2)}) collective-permute-start(f32[4,8,4,128]{3,1,2,0:T(8,128)S(1)} %get-tuple-element.31), channel_id=1, source_target_pairs={{0,4},{4,8},{8,12},{12,16},{16,20},{20,24},{24,28},{1,5},{5,9},{9,... | collective-permute-start | bytes 196616 | tf_op jit(solution)/shard_map/ppermute | solution.py:23
  15.1 0.0 copy-start.16
  16.4 0.6 fusion.111
  17.0 1.3 gather_fusion.1
  18.3 0.0 copy-done.1
  18.3 0.8 gather_fusion
  19.2 0.6 fusion.70
  19.8 0.6 fusion.66
  20.5 1.3 compare_select_fusion.8
  21.8 0.1 broadcast_multiply_fusion.6
  21.9 1.1 broadcast_multiply_fusion.3
  22.9 0.7 add_subtract_fusion
  23.6 0.0 collective-permute-done
  23.6 0.0 collective-permute-done.1
  23.6 0.1 pad_maximum_fusion.2
  23.7 0.4 fusion.107
  24.1 1.1 copy.38
  25.2 0.4 copy.36
  25.6 1.3 collective-permute-start.2
  26.9 4.5 %collective-permute-start.3 = (f32[4,8,72,4]{2,1,3,0:T(8,128)}, f32[4,8,72,4]{2,1,3,0:T(8,128)S(1)}, u32[]{:S(2)}, u32[]{:S(2)}) collective-permute-start(f32[4,8,72,4]{2,1,3,0:T(8,128)} %copy.38), channel_id=1, source_target_pairs={{0,1},{1,2},{2,3},{4,5},{5,6},{6,7},{8,9},{9,10},{10,11},{12,13},{... | collective-permute-start | bytes 110600 | tf_op jit(solution)/shard_map/ppermute | solution.py:23
  31.5 1.7 fusion.68
  33.1 1.8 copy.35
  35.0 0.0 collective-permute-done.3
  35.0 0.5 copy.39
  35.5 0.0 collective-permute-done.2
  35.5 1.4 copy.37
  36.9 1.1 copy-done.3
  38.0 4.3 %select_maximum_fusion.4 = f32[4,16,72,136]{3,1,2,0:T(8,128)} fusion(f32[4,8,72,4]{3,1,2,0:T(8,128)S(1)} %copy.37, f32[4,8,72,4]{3,1,2,0:T(8,128)S(1)} %copy.39, f32[4,8,4,128]{3,1,2,0:T(8,128)S(1)} %collective-permute-done, f32[4,8,64,128]{3,1,2,0:T(8,128)S(1)} %bitcast.115, f32[4,8,4,128]{3,1,2,0:T(8,128)S(1)} %collective-permute-done.1), kind=kLoop, calls=%fused_computation.8 | loop fusion | flops 7520256 | bytes 3760128 | tf_op jit(solution)/shard_map/concatenate | solution.py:21
  42.3 3.9 %pad_maximum_fusion = (f32[4,8,72,132]{3,1,2,0:T(8,128)S(1)}, f32[4,8,72,132]{3,1,2,0:T(8,128)}) fusion(f32[4,8,72,4]{3,1,2,0:T(8,128)} %copy-done.3, f32[4,8,4,128]{3,1,2,0:T(8,128)S(1)} %collective-permute-done, f32[4,8,64,128]{3,1,2,0:T(8,128)S(1)} %bitcast.116, f32[4,8,4,128]{3,1,2,0:T(8,128)S(1)} %collective-permute-done.1, f32[4,8,72,4]{3,1,2,0:T(8,128)} %copy-done.2), kind=kLoop, calls=%fused_computation.13 | loop fusion | flops 1824768 | bytes 3686400 | tf_op jit(solution)/shard_map/concatenate | solution.py:21
  46.3 16.0 %fusion.37 = f32[4,8,64,128]{3,1,2,0:T(8,128)} fusion(f32[4,8,4,128]{3,1,2,0:T(8,128)S(1)} %collective-permute-done.1, f32[4,8,4,128]{3,1,2,0:T(8,128)S(1)} %collective-permute-done, f32[4,16,72,136]{3,1,2,0:T(8,128)} %select_maximum_fusion.4, f32[4,8,72,132]{3,1,2,0:T(8,128)} %get-tuple-element.25, f32[4,8,72,132]{3,1,2,0:T(8,128)S(1)} %get-tuple-element.24, ...), kind=kLoop, calls=%fused_computation.67 | loop fusion | flops 9699328 | bytes 19005440 | tf_op jit(solution)/shard_map/add | solution.py:48
  62.2 1.3 multiply_bitcast_fusion.1
  63.6 3.7 %fusion.61 = f32[4,8,64,128]{3,1,2,0:T(8,128)S(1)} fusion(f32[1,8,64,128]{3,1,2,0:T(8,128)S(1)} %get-tuple-element.19, f32[1,8,64,128]{3,1,2,0:T(8,128)} %get-tuple-element.41, f32[1,8,64,128]{3,1,2,0:T(8,128)S(1)} %get-tuple-element.18, f32[1,8,64,128]{3,1,2,0:T(8,128)} %get-tuple-element.43, f32[1,4,8,64,128]{4,3,2,1,0:T(8,128)} %param.13, ...), kind=kLoop, calls=%fused_computation.108 | loop fusion | flops 2621440 | bytes 5570560 | tf_op jit(solution)/shard_map/div | solution.py:88
  67.3 3.6 %collective-permute-start.4 = (f32[4,8,4,128]{3,1,2,0:T(8,128)S(1)}, f32[4,8,4,128]{3,1,2,0:T(8,128)S(1)}, u32[]{:S(2)}, u32[]{:S(2)}) collective-permute-start(f32[4,8,4,128]{3,1,2,0:T(8,128)S(1)} %get-tuple-element.28), channel_id=1, source_target_pairs={{4,0},{8,4},{12,8},{16,12},{20,16},{24,20},{28,24},{5,1},{9,5},{13... | collective-permute-start | bytes 196616 | tf_op jit(solution)/shard_map/ppermute | solution.py:25
  70.8 2.5 collective-permute-start.5
  73.3 0.1 collective-permute-done.4
  73.4 4.8 %collective-permute-done.5 = f32[4,8,4,128]{3,1,2,0:T(8,128)S(1)} collective-permute-done((f32[4,8,4,128]{3,1,2,0:T(8,128)S(1)}, f32[4,8,4,128]{3,1,2,0:T(8,128)S(1)}, u32[]{:S(2)}, u32[]{:S(2)}) %collective-permute-start.5) | collective-permute-done | bytes 65568 | tf_op jit(solution)/shard_map/ppermute | solution.py:23
  78.2 0.1 pad_maximum_fusion.3
  78.3 1.4 fusion.106
  79.7 1.7 copy.47
  81.4 3.4 %collective-permute-start.7 = (f32[4,8,72,4]{2,1,3,0:T(8,128)S(1)}, f32[4,8,72,4]{2,1,3,0:T(8,128)S(1)}, u32[]{:S(2)}, u32[]{:S(2)}) collective-permute-start(f32[4,8,72,4]{2,1,3,0:T(8,128)S(1)} %copy.47), channel_id=1, source_target_pairs={{0,1},{1,2},{2,3},{4,5},{5,6},{6,7},{8,9},{9,10},{10,11},{12,13},{... | collective-permute-start | bytes 110600 | tf_op jit(solution)/shard_map/ppermute | solution.py:23
  84.8 1.1 copy.45
  85.8 1.3 collective-permute-start.6
  87.1 0.0 collective-permute-done.7
  87.1 0.5 copy.48
  87.6 4.8 %collective-permute-done.6 = f32[4,8,72,4]{2,1,3,0:T(8,128)} collective-permute-done((f32[4,8,72,4]{2,1,3,0:T(8,128)}, f32[4,8,72,4]{2,1,3,0:T(8,128)}, u32[]{:S(2)}, u32[]{:S(2)}) %collective-permute-start.6) | collective-permute-done | bytes 36896 | tf_op jit(solution)/shard_map/ppermute | solution.py:25
  92.4 2.3 copy.46
  94.7 5.5 %select_maximum_fusion = f32[4,16,72,136]{3,1,2,0:T(8,128)} fusion(f32[4,8,72,4]{3,1,2,0:T(8,128)} %copy.46, f32[4,8,72,4]{3,1,2,0:T(8,128)S(1)} %copy.48, f32[4,8,4,128]{3,1,2,0:T(8,128)S(1)} %collective-permute-done.4, f32[4,8,64,128]{3,1,2,0:T(8,128)S(1)} %fusion.61, f32[4,8,4,128]{3,1,2,0:T(8,128)S(1)} %collective-permute-done.5), kind=kLoop, calls=%fused_computation.4 | loop fusion | flops 7520256 | bytes 3760128 | tf_op jit(solution)/shard_map/concatenate | solution.py:21
  100.2 3.0 pad_maximum_fusion.1
  103.2 19.4 %fusion.9 = f32[4,8,64,128]{3,1,2,0:T(8,128)} fusion(f32[4,8,4,128]{3,1,2,0:T(8,128)S(1)} %collective-permute-done.5, f32[4,8,4,128]{3,1,2,0:T(8,128)S(1)} %collective-permute-done.4, f32[4,16,72,136]{3,1,2,0:T(8,128)} %select_maximum_fusion, f32[4,8,72,132]{3,1,2,0:T(8,128)} %get-tuple-element.21, f32[4,8,72,132]{3,1,2,0:T(8,128)} %get-tuple-element.20, ...), kind=kLoop, calls=%fused_computation.39 | loop fusion | flops 9699328 | bytes 19005440 | tf_op jit(solution)/shard_map/add | solution.py:48
  122.7 2.5 fusion.78
  125.2 0.0 all-reduce.5.cloned.1.call-update
  125.2 2.8 fusion.63
  128.0 0.0 copy-start.7
  128.0 1.2 copy.56
  129.2 116.5 %all-reduce.5.cloned.1.call-done = (f32[8,64,128]{2,0,1:T(8,128)}, f32[8,64,128]{2,0,1:T(8,128)}) async-done(((f32[8,64,128]{2,0,1:T(8,128)}, f32[8,64,128]{2,0,1:T(8,128)}), (f32[8,64,128]{2,0,1:T(8,128)}, f32[8,64,128]{2,0,1:T(8,128)})) %all-reduce.5.cloned.1.call-update) | async-done | bytes 524304 | tf_op jit(solution)/shard_map/psum | solution.py:149
  245.7 1.0 broadcast_multiply_fusion.1
  246.7 0.8 copy.57
  247.4 1.7 multiply_reduce_fusion
  249.1 72.9 %psum.23 = f32[]{:T(128)} all-reduce(f32[]{:T(128)} %get-tuple-element.34), channel_id=1, replica_groups=mesh['shot'=16,'gx'=8,'gy'=4] {'gx','gy'}, use_global_device_ids=true, to_apply=%region_3.4 | all-reduce | flops 1 | bytes 8 | tf_op jit(solution)/shard_map/psum | solution.py:150
  322.0 0.8 copy.58
  (42 shorter events, 0.2 us)
Async XLA Ops:
  7.2 9.8 %copy-start = (s32[512]{0:T(512)S(1)}, s32[512]{0:T(512)}, u32[]{:S(2)}) copy-start(s32[512]{0:T(512)} %param.17) | copy-start | bytes 6148
  7.2 9.2 %copy-start.12 = (f32[1,2]{1,0:T(1,128)S(1)}, f32[1,2]{1,0:T(1,128)}, u32[]{:S(2)}) copy-start(f32[1,2]{1,0:T(1,128)} %param.20) | copy-start | bytes 28
  7.2 11.1 %copy-start.1 = (s32[512]{0:T(512)S(1)}, s32[512]{0:T(512)}, u32[]{:S(2)}) copy-start(s32[512]{0:T(512)} %param.16) | copy-start | bytes 6148
  7.2 11.9 %copy-start.11 = (f32[1,2,512]{2,1,0:T(2,128)S(1)}, f32[1,2,512]{2,1,0:T(2,128)}, u32[]{:S(2)}) copy-start(f32[1,2,512]{2,1,0:T(2,128)} %param.23) | copy-start | bytes 12292
  7.2 11.9 %copy-start.13 = (s32[1,512]{1,0:T(1,128)S(1)}, s32[1,512]{1,0:T(1,128)}, u32[]{:S(2)}) copy-start(s32[1,512]{1,0:T(1,128)} %param.22) | copy-start | bytes 6148
  7.2 11.9 %copy-start.14 = (s32[1,512]{1,0:T(1,128)S(1)}, s32[1,512]{1,0:T(1,128)}, u32[]{:S(2)}) copy-start(s32[1,512]{1,0:T(1,128)} %param.21) | copy-start | bytes 6148
  7.2 238.5 %all-reduce.5.cloned.1.call-start = ((), (), s32[]{:S(2)}) async-start(), calls=%async_computation | async-start | bytes 1048576 | tf_op jit(solution)/shard_map/psum | solution.py:149
  9.1 14.5 %collective-permute-start = (f32[4,8,4,128]{3,1,2,0:T(8,128)S(1)}, f32[4,8,4,128]{3,1,2,0:T(8,128)S(1)}, u32[]{:S(2)}, u32[]{:S(2)}) collective-permute-start(f32[4,8,4,128]{3,1,2,0:T(8,128)S(1)} %get-tuple-element.30), channel_id=1, source_target_pairs={{4,0},{8,4},{12,8},{16,12},{20,16},{24,20},{28,24},{5,1},{9,5},{13... | collective-permute-start | bytes 196616 | tf_op jit(solution)/shard_map/ppermute | solution.py:25
  11.5 12.1 %collective-permute-start.1 = (f32[4,8,4,128]{3,1,2,0:T(8,128)S(1)}, f32[4,8,4,128]{3,1,2,0:T(8,128)S(1)}, u32[]{:S(2)}, u32[]{:S(2)}) collective-permute-start(f32[4,8,4,128]{3,1,2,0:T(8,128)S(1)} %get-tuple-element.31), channel_id=1, source_target_pairs={{0,4},{4,8},{8,12},{12,16},{16,20},{20,24},{24,28},{1,5},{5,9},{9,... | collective-permute-start | bytes 196616 | tf_op jit(solution)/shard_map/ppermute | solution.py:23
  15.0 5.4 %copy-start.15 = (s32[64]{0:T(128)}, s32[64]{0:T(128)S(1)}, u32[]{:S(2)}) copy-start(s32[64]{0:T(128)S(1)} %iota_add_fusion.1) | copy-start | bytes 772
  15.1 8.6 %copy-start.16 = (s32[128]{0:T(128)}, s32[128]{0:T(128)S(1)}, u32[]{:S(2)}) copy-start(s32[128]{0:T(128)S(1)} %iota_add_fusion) | copy-start | bytes 1540
  25.6 9.9 %collective-permute-start.2 = (f32[4,8,72,4]{2,1,3,0:T(8,128)S(1)}, f32[4,8,72,4]{2,1,3,0:T(8,128)}, u32[]{:S(2)}, u32[]{:S(2)}) collective-permute-start(f32[4,8,72,4]{2,1,3,0:T(8,128)S(1)} %copy.36), channel_id=1, source_target_pairs={{1,0},{2,1},{3,2},{5,4},{6,5},{7,6},{9,8},{10,9},{11,10},{13,12},{... | collective-permute-start | bytes 110600 | tf_op jit(solution)/shard_map/ppermute | solution.py:25
  26.9 8.1 %collective-permute-start.3 = (f32[4,8,72,4]{2,1,3,0:T(8,128)}, f32[4,8,72,4]{2,1,3,0:T(8,128)S(1)}, u32[]{:S(2)}, u32[]{:S(2)}) collective-permute-start(f32[4,8,72,4]{2,1,3,0:T(8,128)} %copy.38), channel_id=1, source_target_pairs={{0,1},{1,2},{2,3},{4,5},{5,6},{6,7},{8,9},{9,10},{10,11},{12,13},{... | collective-permute-start | bytes 110600 | tf_op jit(solution)/shard_map/ppermute | solution.py:23
  35.4 1.4 copy-start.2
  36.9 1.1 copy-start.3
  67.3 6.2 %collective-permute-start.4 = (f32[4,8,4,128]{3,1,2,0:T(8,128)S(1)}, f32[4,8,4,128]{3,1,2,0:T(8,128)S(1)}, u32[]{:S(2)}, u32[]{:S(2)}) collective-permute-start(f32[4,8,4,128]{3,1,2,0:T(8,128)S(1)} %get-tuple-element.28), channel_id=1, source_target_pairs={{4,0},{8,4},{12,8},{16,12},{20,16},{24,20},{28,24},{5,1},{9,5},{13... | collective-permute-start | bytes 196616 | tf_op jit(solution)/shard_map/ppermute | solution.py:25
  70.8 7.4 %collective-permute-start.5 = (f32[4,8,4,128]{3,1,2,0:T(8,128)S(1)}, f32[4,8,4,128]{3,1,2,0:T(8,128)S(1)}, u32[]{:S(2)}, u32[]{:S(2)}) collective-permute-start(f32[4,8,4,128]{3,1,2,0:T(8,128)S(1)} %get-tuple-element.29), channel_id=1, source_target_pairs={{0,4},{4,8},{8,12},{12,16},{16,20},{20,24},{24,28},{1,5},{5,9},{9,... | collective-permute-start | bytes 196616 | tf_op jit(solution)/shard_map/ppermute | solution.py:23
  81.4 5.8 %collective-permute-start.7 = (f32[4,8,72,4]{2,1,3,0:T(8,128)S(1)}, f32[4,8,72,4]{2,1,3,0:T(8,128)S(1)}, u32[]{:S(2)}, u32[]{:S(2)}) collective-permute-start(f32[4,8,72,4]{2,1,3,0:T(8,128)S(1)} %copy.47), channel_id=1, source_target_pairs={{0,1},{1,2},{2,3},{4,5},{5,6},{6,7},{8,9},{9,10},{10,11},{12,13},{... | collective-permute-start | bytes 110600 | tf_op jit(solution)/shard_map/ppermute | solution.py:23
  85.8 6.6 %collective-permute-start.6 = (f32[4,8,72,4]{2,1,3,0:T(8,128)}, f32[4,8,72,4]{2,1,3,0:T(8,128)}, u32[]{:S(2)}, u32[]{:S(2)}) collective-permute-start(f32[4,8,72,4]{2,1,3,0:T(8,128)} %copy.45), channel_id=1, source_target_pairs={{1,0},{2,1},{3,2},{5,4},{6,5},{7,6},{9,8},{10,9},{11,10},{13,12},{... | collective-permute-start | bytes 110600 | tf_op jit(solution)/shard_map/ppermute | solution.py:25
  94.7 5.5 %copy-start.4 = (f32[4,8,72,4]{3,1,2,0:T(8,128)S(1)}, f32[4,8,72,4]{3,1,2,0:T(8,128)}, u32[]{:S(2)}) copy-start(f32[4,8,72,4]{3,1,2,0:T(8,128)} %copy.46) | copy-start | bytes 110596
  103.2 19.4 %copy-start.5 = (f32[4,8,64,128]{3,1,2,0:T(8,128)S(1)}, f32[4,8,64,128]{3,1,2,0:T(8,128)}, u32[]{:S(2)}) copy-start(f32[4,8,64,128]{3,1,2,0:T(8,128)} %fusion.37) | copy-start | bytes 3145732
  103.2 19.4 %copy-start.10 = (f32[64,128]{1,0:T(8,128)S(1)}, f32[64,128]{1,0:T(8,128)}, u32[]{:S(2)}) copy-start(f32[64,128]{1,0:T(8,128)} %fusion.68) | copy-start | bytes 98308
  122.6 2.6 copy-start.6
  122.6 2.6 copy-start.8
  122.6 2.6 copy-start.9
  128.0 119.4 %copy-start.7 = (f32[8,64,128]{2,1,0:T(8,128)S(1)}, f32[8,64,128]{2,1,0:T(8,128)}, u32[]{:S(2)}) copy-start(f32[8,64,128]{2,1,0:T(8,128)} %param.15) | copy-start | bytes 786436
Sparse Core Ops, SparseCore 0:
  125.3 120.3 all-reduce.4
where the time goes:
time: 332 us; the launch traced here: 331 us
  waiting for transfers between devices  126 us (38%)
  blocking collectives  72.9 us (22%)
  other arithmetic  68.5 us (21%)
  starting transfers between devices  22.4 us (7%)
  local copies, waits for them, and re-layouts  20.8 us (6%)
  between operations  17.6 us (5%)
    psum x1, waiting for transfers between devices, local(): grad_sum, hess_sum = lax.psum((grad_part, hess_part), 'shot')  116 us
    psum x1, blocking collectives, local(): lax.psum(jnp.sum(born_dir * hess_sum), ('gx', 'gy')) / shots_total  72.9 us
    add x2, other arithmetic, laplace(): summed = summed + COEFS[offset] * neighbours  35.4 us
    concatenate x6, other arithmetic, with_halo(): jnp.concatenate([lax.ppermute(tail, axis, [(i, (i + 1) % count) for i in...  16.9 us
    ppermute x4, starting transfers between devices, with_halo(): lax.ppermute(tail, axis, [(i, (i + 1) % count) for i in range(ends)])  13.9 us
    ppermute x4, starting transfers between devices, with_halo(): lax.ppermute(head, axis, [((i + 1) % count, i) for i in range(ends)])  8.5 us
    unnamed x39, local copies, waits for them, and re-layouts  7.48 us
  transfers between devices with their start and end apart: 9, of which 4 were waited for; matrix products, arithmetic and copies ran while one was open for 5% of the time, Pallas kernels for 0%

commit v1 on v0

v1 whole, which is shorter than its diff:
```python
import functools
import math

import jax
import jax.numpy as jnp
from jax import lax
from jax.experimental import pallas as pl
from jax.experimental.pallas import tpu as pltpu
from jax.sharding import PartitionSpec as P

PML_W = 16
COEFS = (-205.0 / 72.0, 8.0 / 5.0, -1.0 / 5.0, 8.0 / 315.0, -1.0 / 560.0)
LEVELS = 8
ROWS = 64
COLS = 128
BLOCKS = ROWS // 8
MESH = pl.DeviceIdType.MESH


def kernel(
    sizes,
    now_ref,
    before_ref,
    speed_ref,
    born_ref,
    pml_x_ref,
    pml_y_ref,
    src_x_ref,
    src_y_ref,
    amp_ref,
    rec_x_ref,
    rec_y_ref,
    res_ref,
    out_ref,
    sums_ref,
    curv_ref,
    field0,
    field1,
    prev,
    speed,
    born,
    terms,
    sib,
    up_sum,
    down_sum,
    x_send,
    x_recv,
    y_send,
    y_recv,
    merged,
    planes,
    curv_sib,
    curv_y,
    curv_x,
    curv_z,
    in_sems,
    x_sems,
    y_sems,
    out_sem,
    sib_sems,
    rs_sems,
    ag_sems,
    agsib_sems,
    cs_sems,
    cy_sems,
    cx_sems,
    cz_sems,
):
    shots, n_x, n_y = sizes
    n_z = shots // 2
    reach = n_z // 2
    per = LEVELS // n_z
    shot = lax.axis_index("shot")
    core = lax.rem(shot, 2)
    z = shot // 2
    gx = lax.axis_index("gx")
    gy = lax.axis_index("gy")

    def z_id(k):
        return {"shot": lax.rem(z + k + 2 * n_z, n_z) * 2 + core}

    def x_id(k):
        return {"gx": lax.rem(gx + k + n_x, n_x)}

    def y_id(k):
        return {"gy": lax.rem(gy + k + n_y, n_y)}

    sib_id = {"shot": 2 * z + 1 - core}

    def remote(src, dst, send, recv, who):
        return pltpu.make_async_remote_copy(
            src_ref=src, dst_ref=dst, send_sem=send, recv_sem=recv, device_id=who, device_id_type=MESH
        )

    loads = [
        pltpu.make_async_copy(now_ref.at[0], field0.at[:, :, pl.ds(8, ROWS), :], in_sems.at[0]),
        pltpu.make_async_copy(before_ref.at[0], prev, in_sems.at[1]),
        pltpu.make_async_copy(speed_ref, speed, in_sems.at[2]),
        pltpu.make_async_copy(born_ref, born, in_sems.at[3]),
    ]
    for load in loads:
        load.start()

    barrier = pltpu.get_barrier_semaphore()
    partners = [sib_id]
    partners += [z_id(k) for k in range(1, n_z)]
    partners += [x_id(k) for k in range(1, n_x)]
    partners += [y_id(k) for k in range(1, n_y)]
    for who in partners:
        pl.semaphore_signal(barrier, inc=1, device_id=who, device_id_type=MESH)

    row0 = gx * ROWS
    col0 = gy * COLS
    whole_x = n_x * ROWS
    whole_y = n_y * COLS
    row = row0 + lax.broadcasted_iota(jnp.int32, (ROWS, COLS), 0)
    col = col0 + lax.broadcasted_iota(jnp.int32, (ROWS, COLS), 1)

    def layer(place, length, far):
        value = jnp.maximum(jnp.maximum(PML_W - place, far - (length - 1 - place)), 0)
        return value.astype(jnp.float32) / PML_W

    layer_x = layer(row, whole_x, pml_x_ref[whole_x - 1])
    layer_y = layer(col, whole_y, pml_y_ref[whole_y - 1])
    damp = layer_x * layer_x + layer_y * layer_y
    inverse = 1.0 / (1.0 + damp)
    planes[0] = inverse
    planes[1] = (1.0 - damp) * inverse
    at_source = (row == src_x_ref[0]) & (col == src_y_ref[0])
    planes[2] = jnp.where(at_source, amp_ref[0, 0], 0.0)
    planes[3] = jnp.where(at_source, amp_ref[0, 1], 0.0)
    count_rec = rec_x_ref.shape[1]
    hot_x = rec_x_ref[...] == row0 + lax.broadcasted_iota(jnp.int32, (ROWS, count_rec), 0)
    hot_y = rec_y_ref[...] == col0 + lax.broadcasted_iota(jnp.int32, (COLS, count_rec), 0)
    weights = [jnp.ones((1, count_rec), jnp.float32)]
    for turn in range(2):
        rest = res_ref[0, turn : turn + 1, :]
        for _ in range(3):
            head = rest.astype(jnp.bfloat16).astype(jnp.float32)
            weights.append(head)
            rest = rest - head
    left = jnp.concatenate([jnp.where(hot_x, w, 0.0).astype(jnp.bfloat16) for w in weights], axis=0)
    right = jnp.where(hot_y, 1.0, 0.0).astype(jnp.bfloat16)
    hits = lax.dot_general(
        left, right, (((1,), (1,)), ((), ())), preferred_element_type=jnp.float32
    )
    parts = [hits[i * ROWS : (i + 1) * ROWS] for i in range(7)]
    planes[4] = parts[1] + parts[2] + parts[3]
    planes[5] = parts[4] + parts[5] + parts[6]
    planes[6] = parts[0]

    lane = lax.broadcasted_iota(jnp.int32, (8, COLS), 1)
    low_half = (lane & 4) == 0
    group = lane // 8

    def block(b):
        return pl.ds(pl.multiple_of(b * 8, 8), 8)

    def inner(b, shift=0):
        return pl.ds(pl.multiple_of(b * 8, 8) + (8 + shift), 8)

    def pack_x(field):
        for f in range(4):
            for lev in range(LEVELS):
                x_send[0, f * 8 + lev] = field[f, lev, 8:12, :]
                x_send[1, f * 8 + lev] = field[f, lev, ROWS + 4 : ROWS + 8, :]

    def pack_y(field):
        def body(b, carry):
            packed = []
            for pair in range(2):
                total = jnp.zeros((8, COLS), jnp.float32)
                for i in range(16):
                    value = field[2 * pair + i // 8, i % 8, inner(b), :]
                    rolled = pltpu.roll(value, (8 * i + 4) % COLS, 1)
                    total = jnp.where(group == i, rolled, total)
                packed.append(total)
            y_send[0, block(b), :] = jnp.where(low_half, packed[0], pltpu.roll(packed[1], 4, 1))
            y_send[1, block(b), :] = jnp.where(low_half, pltpu.roll(packed[0], COLS - 4, 1), packed[1])
            return carry

        lax.fori_loop(0, BLOCKS, body, 0)

    def halo_copies(turn):
        return [
            remote(x_send.at[0], x_recv.at[turn, 0], x_sems.at[0, turn, 0], x_sems.at[1, turn, 0], x_id(-1)),
            remote(x_send.at[1], x_recv.at[turn, 1], x_sems.at[0, turn, 1], x_sems.at[1, turn, 1], x_id(1)),
            remote(y_send.at[0], y_recv.at[turn, 0], y_sems.at[0, turn, 0], y_sems.at[1, turn, 0], y_id(1)),
            remote(y_send.at[1], y_recv.at[turn, 1], y_sems.at[0, turn, 1], y_sems.at[1, turn, 1], y_id(-1)),
        ]

    def unpack(field, turn):
        for f in range(4):
            for lev in range(LEVELS):
                below = x_recv[turn, 0, f * 8 + lev]
                above = x_recv[turn, 1, f * 8 + lev]
                field[f, lev, 4:8, :] = jnp.where(gx == 0, 0.0, above)
                field[f, lev, ROWS + 8 : ROWS + 12, :] = jnp.where(gx == n_x - 1, 0.0, below)
        for b in range(BLOCKS):
            rows = pl.ds(b * 8, 8)
            tails = jnp.where(gy == 0, 0.0, y_recv[turn, 0, rows, :])
            heads = jnp.where(gy == n_y - 1, 0.0, y_recv[turn, 1, rows, :])
            merged[0, rows, :] = jnp.where(low_half, heads, pltpu.roll(tails, COLS - 4, 1))
            merged[1, rows, :] = jnp.where(
                low_half, pltpu.roll(heads, COLS - 4, 1), pltpu.roll(tails, COLS - 8, 1)
            )

    def laplace(field, f, b, centre, sides):
        results = []
        for lev in range(LEVELS):
            own = centre[lev]
            at = (8 * (f % 2) + lev) * 8
            side = pltpu.roll(sides, (COLS - at) % COLS, 1) if at else sides
            total = (3.0 * COEFS[0]) * own
            for k in range(1, 5):
                near = field[f, lev, inner(b, k), :] + field[f, lev, inner(b, -k), :]
                near += pltpu.roll(jnp.where(lane < k, side, own), COLS - k, 1)
                near += pltpu.roll(jnp.where(lane >= COLS - k, side, own), k, 1)
                if lev + k < LEVELS:
                    near += centre[lev + k]
                if lev - k >= 0:
                    near += centre[lev - k]
                total += COEFS[k] * near
            results.append(total)
        return results

    def old(turn, f, lev, b):
        return prev[f, lev, block(b), :] if turn == 0 else field0[f, lev, inner(b), :]

    def put(turn, f, lev, b, value):
        if turn == 0:
            field1[f, lev, inner(b), :] = value
        else:
            prev[f, lev, block(b), :] = value

    def incident(turn, field):
        def body(b, curv):
            sides = merged[0, block(b), :]
            u = [field[0, lev, inner(b), :] for lev in range(LEVELS)]
            du = [field[1, lev, inner(b), :] for lev in range(LEVELS)]
            lap_u = laplace(field, 0, b, u, sides)
            lap_du = laplace(field, 1, b, du, sides)
            inv = planes[0, block(b), :]
            fade = planes[1, block(b), :]
            for lev in range(LEVELS):
                lam = field[2, lev, inner(b), :]
                dlam = field[3, lev, inner(b), :]
                grad = lam * lap_u[lev]
                hess = dlam * lap_u[lev] + lam * lap_du[lev]
                if turn == 1:
                    grad += terms[0, lev, block(b), :]
                    hess += terms[1, lev, block(b), :]
                terms[0, lev, block(b), :] = grad
                terms[1, lev, block(b), :] = hess
                direction = born[lev, block(b), :]
                if turn == 1:
                    curv += direction * hess
                pace = speed[lev, block(b), :]
                new_u = 2.0 * u[lev] + pace * lap_u[lev]
                if lev == 1:
                    new_u += planes[2 + turn, block(b), :]
                new_du = 2.0 * du[lev] + pace * lap_du[lev] + direction * lap_u[lev]
                put(turn, 0, lev, b, new_u * inv - fade * old(turn, 0, lev, b))
                put(turn, 1, lev, b, new_du * inv - fade * old(turn, 1, lev, b))
            return curv

        return lax.fori_loop(0, BLOCKS, body, jnp.zeros((8, COLS), jnp.float32))

    def adjoint(turn, field):
        def body(b, carry):
            sides = merged[1, block(b), :]
            lam = [field[2, lev, inner(b), :] for lev in range(LEVELS)]
            dlam = [field[3, lev, inner(b), :] for lev in range(LEVELS)]
            lap_lam = laplace(field, 2, b, lam, sides)
            lap_dlam = laplace(field, 3, b, dlam, sides)
            inv = planes[0, block(b), :]
            fade = planes[1, block(b), :]
            for lev in range(LEVELS):
                pace = speed[lev, block(b), :]
                new_lam = 2.0 * lam[lev] + pace * lap_lam[lev]
                new_dlam = 2.0 * dlam[lev] + pace * lap_dlam[lev] + born[lev, block(b), :] * lap_lam[lev]
                if lev == 1:
                    new_lam += planes[4 + turn, block(b), :]
                    new_dlam += planes[6, block(b), :] * field[1, lev, inner(b), :]
                put(turn, 2, lev, b, new_lam * inv - fade * old(turn, 2, lev, b))
                put(turn, 3, lev, b, new_dlam * inv - fade * old(turn, 3, lev, b))
            return carry

        lax.fori_loop(0, BLOCKS, body, 0)

    loads[0].wait()
    pack_y(field0)
    pack_x(field0)
    pl.semaphore_wait(barrier, len(partners))
    copies = halo_copies(0)
    for copy in copies:
        copy.start()
    for load in loads[1:]:
        load.wait()
    for copy in copies:
        copy.wait()
    unpack(field0, 0)
    incident(0, field0)
    adjoint(0, field0)

    pack_y(field1)
    pack_x(field1)
    copies = halo_copies(1)
    for copy in copies:
        copy.start()
    for copy in copies:
        copy.wait()
    unpack(field1, 1)
    curv = incident(1, field1)

    swap = remote(terms.at[1 - core], sib, sib_sems.at[0], sib_sems.at[1], sib_id)
    swap.start()
    curv_sib[core] = curv
    curv_swap = remote(curv_sib.at[core], curv_sib.at[core], cs_sems.at[0], cs_sems.at[1], sib_id)
    curv_swap.start()

    def spread(buffer, place, value, sems, ident, count):
        buffer[place] = value
        sent = [
            remote(buffer.at[place], buffer.at[place], sems.at[0, k - 1], sems.at[1, k - 1], ident(k))
            for k in range(1, count)
        ]
        for copy in sent:
            copy.start()
        return sent

    def gather(sent, buffer, count):
        for copy in sent:
            copy.wait()
        total = buffer[0]
        for k in range(1, count):
            total = total + buffer[k]
        return total

    curv_swap.wait()
    curv = curv_sib[0] + curv_sib[1]
    sent_y = spread(curv_x, gx, curv, cx_sems, x_id, n_x)

    adjoint(1, field1)
    save = pltpu.make_async_copy(prev, out_ref.at[0], out_sem)
    save.start()

    def owner(k):
        return pl.ds(lax.rem(z + k + 2 * n_z, n_z) * per, per)

    halves = (pl.ds(0, ROWS // 2), pl.ds(ROWS // 2, ROWS // 2))
    full = pl.ds(0, ROWS)
    sums = (up_sum, down_sum)
    signs = (1, -1)

    def add(level, rows, *others):
        total = terms[core, level, rows, :]
        for other in others:
            total = total + other
        terms[core, level, rows, :] = total

    swap.wait()
    sent = []
    waiting = [None, None]
    for way in range(2):
        level = owner(reach)
        add(level, halves[way], sib[level, halves[way], :])
        copy = remote(
            terms.at[core, level, halves[way], :],
            sums[way].at[0, :, halves[way], :],
            rs_sems.at[0, way, 0],
            rs_sems.at[1, way, 0],
            z_id(signs[way]),
        )
        copy.start()
        waiting[way] = copy
        sent.append(copy)
    for k in range(1, reach):
        for way in range(2):
            level = owner(signs[way] * k)
            add(level, full, sib[level, full, :])
    add(owner(0), full, sib[owner(0), full, :])
    for step in range(1, reach):
        for way in range(2):
            waiting[way].wait_recv()
            rows = halves[way] if step == 1 else full
            level = owner(signs[way] * (reach - step))
            add(level, rows, sums[way][step - 1, :, rows, :])
            copy = remote(
                terms.at[core, level, full, :],
                sums[way].at[step, :, full, :],
                rs_sems.at[0, way, step],
                rs_sems.at[1, way, step],
                z_id(signs[way]),
            )
            copy.start()
            waiting[way] = copy
            sent.append(copy)
        if step == 1:
            curv = gather(sent_y, curv_x, n_x)
            sent_x = spread(curv_y, gy, curv, cy_sems, y_id, n_y)
        if step == 2:
            curv = gather(sent_x, curv_y, n_y)
            sent_z = spread(curv_z, z, curv, cz_sems, z_id, n_z)
    if reach == 1:
        curv = gather(sent_y, curv_x, n_x)
        sent_x = spread(curv_y, gy, curv, cy_sems, y_id, n_y)
    if reach <= 2:
        curv = gather(sent_x, curv_y, n_y)
        sent_z = spread(curv_z, z, curv, cz_sems, z_id, n_z)
    for way in range(2):
        waiting[way].wait_recv()
        rows = halves[way] if reach == 1 else full
        add(owner(0), rows, sums[way][reach - 1, :, rows, :])
    for copy in sent:
        copy.wait_send()
    sums_ref[core, owner(0)] = terms[core, owner(0)] * (1.0 / shots)

    sent = []
    across = []

    def to_sibling(level, rows, slot):
        copy = remote(
            sums_ref.at[core, level, rows, :],
            sums_ref.at[core, level, rows, :],
            agsib_sems.at[0, slot],
            agsib_sems.at[1, slot],
            sib_id,
        )
        copy.start()
        across.append(copy)

    for step in range(reach):
        for way in range(2):
            if step:
                waiting[way].wait_recv()
            rows = halves[way] if step == reach - 1 else full
            level = owner(-signs[way] * step)
            copy = remote(
                sums_ref.at[core, level, rows, :],
                sums_ref.at[core, level, rows, :],
                ag_sems.at[0, way, step],
                ag_sems.at[1, way, step],
                z_id(signs[way]),
            )
            copy.start()
            waiting[way] = copy
            sent.append(copy)
        if step == 0:
            to_sibling(owner(0), full, 0)
        else:
            for way in range(2):
                to_sibling(owner(-signs[way] * step), full, 2 * step - 1 + way)
    curv = gather(sent_z, curv_z, n_z)
    cells = LEVELS * whole_x * whole_y
    curv_ref[0, 0] = jnp.sum(curv) * (1.0 / (shots * math.sqrt(cells)))
    for way in range(2):
        waiting[way].wait_recv()
        to_sibling(owner(reach), halves[way], 2 * reach - 1 + way)
    for copy in sent:
        copy.wait_send()
    for copy in across:
        copy.wait()
    save.wait()


def local(sizes, *args):
    shots, n_x, n_y = sizes
    n_z = shots // 2
    reach = n_z // 2
    per = LEVELS // n_z
    any_space = pl.BlockSpec(memory_space=pl.ANY)
    smem = pl.BlockSpec(memory_space=pltpu.SMEM)
    vmem = pl.BlockSpec(memory_space=pltpu.VMEM)
    f32 = jnp.float32
    dma = pltpu.SemaphoreType.DMA
    tile = (8, COLS)
    fields, sums, curv = pl.pallas_call(
        functools.partial(kernel, sizes),
        out_shape=(
            jax.ShapeDtypeStruct((1, 4, LEVELS, ROWS, COLS), f32),
            jax.ShapeDtypeStruct((2, LEVELS, ROWS, COLS), f32),
            jax.ShapeDtypeStruct((1, 1), f32),
        ),
        in_specs=[any_space] * 4 + [smem] * 5 + [vmem] * 3,
        out_specs=(any_space, vmem, smem),
        scratch_shapes=[
            pltpu.VMEM((4, LEVELS, ROWS + 16, COLS), f32),
            pltpu.VMEM((4, LEVELS, ROWS + 16, COLS), f32),
            pltpu.VMEM((4, LEVELS, ROWS, COLS), f32),
            pltpu.VMEM((LEVELS, ROWS, COLS), f32),
            pltpu.VMEM((LEVELS, ROWS, COLS), f32),
            pltpu.VMEM((2, LEVELS, ROWS, COLS), f32),
            pltpu.VMEM((LEVELS, ROWS, COLS), f32),
            pltpu.VMEM((reach, per, ROWS, COLS), f32),
            pltpu.VMEM((reach, per, ROWS, COLS), f32),
            pltpu.VMEM((2, 32, 4, COLS), f32),
            pltpu.VMEM((2, 2, 32, 4, COLS), f32),
            pltpu.VMEM((2, ROWS, COLS), f32),
            pltpu.VMEM((2, 2, ROWS, COLS), f32),
            pltpu.VMEM((2, ROWS, COLS), f32),
            pltpu.VMEM((7, ROWS, COLS), f32),
            pltpu.VMEM((2,) + tile, f32),
            pltpu.VMEM((n_y,) + tile, f32),
            pltpu.VMEM((n_x,) + tile, f32),
            pltpu.VMEM((n_z,) + tile, f32),
            dma((4,)),
            dma((2, 2, 2)),
            dma((2, 2, 2)),
            dma,
            dma((2,)),
            dma((2, 2, reach)),
            dma((2, 2, reach)),
            dma((2, 2 * reach + 1)),
            dma((2,)),
            dma((2, n_y - 1)),
            dma((2, n_x - 1)),
            dma((2, n_z - 1)),
        ],
        compiler_params=pltpu.CompilerParams(
            collective_id=0, has_side_effects=True, vmem_limit_bytes=32 * 1024 * 1024
        ),
    )(*args)
    return fields, sums[0], sums[1], curv[0, 0]


def solution(mesh):
    sizes = (mesh.shape["shot"], mesh.shape["gx"], mesh.shape["gy"])
    placed = (
        P("shot", None, None, "gx", "gy"),
        P("shot", None, None, "gx", "gy"),
        P(None, "gx", "gy"),
        P(None, "gx", "gy"),
        P(),
        P(),
        P("shot"),
        P("shot"),
        P("shot", None),
        P("shot", None),
        P("shot", None),
        P("shot", None, None),
    )
    return jax.shard_map(
        functools.partial(local, sizes),
        mesh=mesh,
        in_specs=placed,
        out_specs=(
            P("shot", None, None, "gx", "gy"),
            P(None, "gx", "gy"),
            P(None, "gx", "gy"),
            P(),
        ),
        check_vma=False,
    )
```

time: 332 us -> 77.2 us (0.23)
  the two profiles are of different devices: /device:TPU:32 before, /device:TPU:1 now
where the time goes in v1:
time: 77.2 us; the launch traced here: 76.8 us
  Pallas kernels  64.1 us (83%)
  local copies, waits for them, and re-layouts  8.88 us (12%)
  between operations  3.76 us (5%)
    pallas_call x1, Pallas kernels, local(): pl.pallas_call(functools.partial(kernel, sizes), out_shape=(jax.ShapeDtyp...  64.1 us
    unnamed x21, local copies, waits for them, and re-layouts  8.05 us

profile of v1, /device:TPU:1, one launch (start us, length us, event | category | flops | bytes accessed | tf_op | source)
XLA Modules:
  0.0 76.8 jit_solution(13995854837322760271)
XLA Ops:
  0.6 0.0 copy-start.5
  1.3 0.0 copy-start.9
  2.0 0.0 copy-done.5
  2.0 0.0 copy-done.9
  2.0 0.0 copy-start
  2.0 1.2 %copy-done = f32[1,4,8,64,128]{4,3,2,1,0:T(8,128)S(1)} copy-done((f32[1,4,8,64,128]{4,3,2,1,0:T(8,128)S(1)}, f32[1,4,8,64,128]{4,3,2,1,0:T(8,128)}, u32[]{:S(2)}) %copy-start) | copy-done | bytes 1048600
  3.2 0.0 copy-start.1
  3.2 1.2 %copy-done.1 = f32[1,4,8,64,128]{4,3,2,1,0:T(8,128)S(1)} copy-done((f32[1,4,8,64,128]{4,3,2,1,0:T(8,128)S(1)}, f32[1,4,8,64,128]{4,3,2,1,0:T(8,128)}, u32[]{:S(2)}) %copy-start.1) | copy-done | bytes 1048600
  4.4 0.0 copy-start.2
  4.4 0.9 %copy-done.2 = f32[8,64,128]{2,1,0:T(8,128)S(1)} copy-done((f32[8,64,128]{2,1,0:T(8,128)S(1)}, f32[8,64,128]{2,1,0:T(8,128)}, u32[]{:S(2)}) %copy-start.2) | copy-done | bytes 262168
  5.4 0.0 copy-start.3
  5.4 0.9 %copy-done.3 = f32[8,64,128]{2,1,0:T(8,128)S(1)} copy-done((f32[8,64,128]{2,1,0:T(8,128)S(1)}, f32[8,64,128]{2,1,0:T(8,128)}, u32[]{:S(2)}) %copy-start.3) | copy-done | bytes 262168
  6.3 0.0 copy-start.4
  6.3 0.7 copy-done.4
  7.0 0.0 copy-start.6
  7.0 0.7 copy-done.6
  7.7 0.0 copy-start.7
  7.7 0.7 copy-done.7
  8.4 0.0 copy-start.8
  8.4 0.7 copy-done.8
  9.1 64.1 %shard_map.147 = (f32[1,4,8,64,128]{4,3,2,1,0:T(8,128)S(1)}, f32[2,8,64,128]{3,2,1,0:T(8,128)S(1)}, f32[1,1]{1,0:T(1,128)}) custom-call(f32[1,4,8,64,128]{4,3,2,1,0:T(8,128)S(1)} %copy-done, f32[1,4,8,64,128]{4,3,2,1,0:T(8,128)S(1)} %copy-done.1, f32[8,64,128]{2,1,0:T(8,128)S(1)} %copy-done.2, f32[8,64,128]{2,1,0:T(8,128)S(1)} %copy-done.3, ...), custom_call_target="tpu_custom_call" | custom-call | tf_op jit(solution)/shard_map/pallas_call | solution.py:478
  73.2 0.8 %slice_bitcast_fusion = (f32[8,64,128]{2,1,0:T(8,128)}, f32[8,64,128]{2,1,0:T(8,128)}) fusion(f32[2,8,64,128]{3,2,1,0:T(8,128)S(1)} %get-tuple-element.8), kind=kLoop, calls=%fused_computation | loop fusion | bytes 1048576 | tf_op jit(solution)/shard_map/squeeze | solution.py:524
  74.0 1.0 %copy.20 = f32[1,4,8,64,128]{4,3,2,1,0:T(8,128)} copy(f32[1,4,8,64,128]{4,3,2,1,0:T(8,128)S(1)} %get-tuple-element.16) | data formatting | bytes 2097152
Async XLA Ops:
  0.6 1.3 %copy-start.5 = (s32[512]{0:T(512)S(1)}, s32[512]{0:T(512)}, u32[]{:S(2)}) copy-start(s32[512]{0:T(512)} %pml_x_ref.1) | copy-start | bytes 6148
  1.3 0.7 copy-start.9
  2.0 1.2 %copy-start = (f32[1,4,8,64,128]{4,3,2,1,0:T(8,128)S(1)}, f32[1,4,8,64,128]{4,3,2,1,0:T(8,128)}, u32[]{:S(2)}) copy-start(f32[1,4,8,64,128]{4,3,2,1,0:T(8,128)} %now_ref.1) | copy-start | bytes 3145732
  3.2 1.2 %copy-start.1 = (f32[1,4,8,64,128]{4,3,2,1,0:T(8,128)S(1)}, f32[1,4,8,64,128]{4,3,2,1,0:T(8,128)}, u32[]{:S(2)}) copy-start(f32[1,4,8,64,128]{4,3,2,1,0:T(8,128)} %before_ref.1) | copy-start | bytes 3145732
  4.4 0.9 %copy-start.2 = (f32[8,64,128]{2,1,0:T(8,128)S(1)}, f32[8,64,128]{2,1,0:T(8,128)}, u32[]{:S(2)}) copy-start(f32[8,64,128]{2,1,0:T(8,128)} %speed_ref.1) | copy-start | bytes 786436
  5.4 0.9 %copy-start.3 = (f32[8,64,128]{2,1,0:T(8,128)S(1)}, f32[8,64,128]{2,1,0:T(8,128)}, u32[]{:S(2)}) copy-start(f32[8,64,128]{2,1,0:T(8,128)} %born_ref.1) | copy-start | bytes 786436
  6.3 0.7 copy-start.4
  7.0 0.7 copy-start.6
  7.7 0.7 copy-start.7
  8.4 0.7 copy-start.8

commit v2 on v1

v2 whole, which is shorter than its diff:
```python
import functools
import math

import jax
import jax.numpy as jnp
import ml_dtypes
import numpy as np
from jax import lax
from jax.experimental import pallas as pl
from jax.experimental.pallas import tpu as pltpu
from jax.sharding import PartitionSpec as P

PML_W = 16
COEFS = (-205.0 / 72.0, 8.0 / 5.0, -1.0 / 5.0, 8.0 / 315.0, -1.0 / 560.0)
LEVELS = 8
ROWS = 64
COLS = 128
BLOCKS = ROWS // 8
MESH = pl.DeviceIdType.MESH


def rounded(value):
    return float(np.asarray(value, ml_dtypes.bfloat16))


HEADS = tuple(rounded(c) for c in COEFS)
RESTS = tuple(rounded(c - h) for c, h in zip(COEFS, HEADS))


def kernel(
    sizes,
    now_ref,
    before_ref,
    speed_ref,
    born_ref,
    pml_x_ref,
    pml_y_ref,
    src_x_ref,
    src_y_ref,
    amp_ref,
    rec_x_ref,
    rec_y_ref,
    res_ref,
    out_ref,
    sums_ref,
    curv_ref,
    field0,
    field1,
    prev,
    speed,
    born,
    terms,
    sib,
    lap,
    band,
    corner,
    join,
    direct,
    x_send,
    x_recv,
    y_send,
    y_recv,
    edge,
    sides,
    planes,
    curv_sib,
    curv_y,
    curv_x,
    curv_z,
    far_x,
    far_y,
    at_x,
    at_y,
    pulse,
    recs_x,
    recs_y,
    weigh,
    in_sems,
    small_sems,
    x_sems,
    y_sems,
    out_sem,
    sib_sems,
    rs_sems,
    ag_sems,
    agsib_sems,
    last_sems,
    cs_sems,
    cy_sems,
    cx_sems,
    cz_sems,
):
    shots, n_x, n_y = sizes
    n_z = shots // 2
    reach = n_z // 2
    per = LEVELS // n_z
    shot = lax.axis_index("shot")
    core = lax.rem(shot, 2)
    z = shot // 2
    gx = lax.axis_index("gx")
    gy = lax.axis_index("gy")

    def z_id(k):
        return {"shot": lax.rem(z + k + 2 * n_z, n_z) * 2 + core}

    def cross_id(k):
        return {"shot": lax.rem(z + k + 2 * n_z, n_z) * 2 + 1 - core}

    def x_id(k):
        return {"gx": lax.rem(gx + k + n_x, n_x)}

    def y_id(k):
        return {"gy": lax.rem(gy + k + n_y, n_y)}

    sib_id = {"shot": 2 * z + 1 - core}

    def remote(src, dst, send, recv, who):
        return pltpu.make_async_remote_copy(
            src_ref=src, dst_ref=dst, send_sem=send, recv_sem=recv, device_id=who, device_id_type=MESH
        )

    loads = [
        pltpu.make_async_copy(now_ref.at[0], field0.at[:, :, pl.ds(8, ROWS), :], in_sems.at[0]),
        pltpu.make_async_copy(before_ref.at[0], prev, in_sems.at[1]),
        pltpu.make_async_copy(speed_ref, speed, in_sems.at[2]),
        pltpu.make_async_copy(born_ref, born, in_sems.at[3]),
    ]
    small = [
        pltpu.make_async_copy(source, target, small_sems.at[i])
        for i, (source, target) in enumerate(
            [
                (pml_x_ref, far_x),
                (pml_y_ref, far_y),
                (src_x_ref, at_x),
                (src_y_ref, at_y),
                (amp_ref, pulse),
                (rec_x_ref, recs_x),
                (rec_y_ref, recs_y),
                (res_ref, weigh),
            ]
        )
    ]
    for load in [loads[0]] + small + loads[1:]:
        load.start()

    barrier = pltpu.get_barrier_semaphore()
    partners = [sib_id]
    partners += [z_id(k) for k in range(1, n_z)]
    partners += [cross_id(1), cross_id(-1)]
    partners += [x_id(k) for k in range(1, n_x)]
    partners += [y_id(k) for k in range(1, n_y)]
    for who in partners:
        pl.semaphore_signal(barrier, inc=1, device_id=who, device_id_type=MESH)

    whole_x = n_x * ROWS
    whole_y = n_y * COLS

    def build_planes():
        for load in small:
            load.wait()
        row0 = gx * ROWS
        col0 = gy * COLS
        row = row0 + lax.broadcasted_iota(jnp.int32, (ROWS, COLS), 0)
        col = col0 + lax.broadcasted_iota(jnp.int32, (ROWS, COLS), 1)

        def layer(place, length, far):
            value = jnp.maximum(jnp.maximum(PML_W - place, far - (length - 1 - place)), 0)
            return value.astype(jnp.float32) / PML_W

        layer_x = layer(row, whole_x, far_x[whole_x - 1])
        layer_y = layer(col, whole_y, far_y[whole_y - 1])
        damp = layer_x * layer_x + layer_y * layer_y
        inverse = 1.0 / (1.0 + damp)
        planes[0] = inverse
        planes[1] = (1.0 - damp) * inverse
        at_source = (row == at_x[0]) & (col == at_y[0])
        planes[2] = jnp.where(at_source, pulse[0, 0], 0.0)
        planes[3] = jnp.where(at_source, pulse[0, 1], 0.0)
        count_rec = recs_x.shape[1]
        hot_x = recs_x[...] == row0 + lax.broadcasted_iota(jnp.int32, (ROWS, count_rec), 0)
        hot_y = recs_y[...] == col0 + lax.broadcasted_iota(jnp.int32, (COLS, count_rec), 0)
        weights = [jnp.ones((1, count_rec), jnp.float32)]
        for turn in range(2):
            rest = weigh[0, turn : turn + 1, :]
            for _ in range(3):
                head = rest.astype(jnp.bfloat16).astype(jnp.float32)
                weights.append(head)
                rest = rest - head
        left = jnp.concatenate([jnp.where(hot_x, w, 0.0).astype(jnp.bfloat16) for w in weights], axis=0)
        right = jnp.where(hot_y, 1.0, 0.0).astype(jnp.bfloat16)
        hits = lax.dot_general(
            left, right, (((1,), (1,)), ((), ())), preferred_element_type=jnp.float32
        )
        parts = [hits[i * ROWS : (i + 1) * ROWS] for i in range(7)]
        planes[4] = parts[1] + parts[2] + parts[3]
        planes[5] = parts[4] + parts[5] + parts[6]
        planes[6] = parts[0]

    lane = lax.broadcasted_iota(jnp.int32, (8, COLS), 1)
    low_half = (lane & 4) == 0
    group = lane // 8

    def build_weights():
        shape = (2 * COLS, 2 * COLS)
        row = lax.broadcasted_iota(jnp.int32, shape, 0)
        col = lax.broadcasted_iota(jnp.int32, shape, 1)
        second = col >= COLS
        row = row & (COLS - 1)
        col = col & (COLS - 1)
        away = jnp.abs(row - col)
        ahead = (col - row) & (COLS - 1)
        ahead = jnp.where((row & 4) != 0, ahead, COLS - ahead)
        crosses = (row & 4) != (col & 4)
        near = jnp.zeros(shape, jnp.float32)
        far = jnp.zeros(shape, jnp.float32)
        for k in range(1, 5):
            value = jnp.where(second, RESTS[k], HEADS[k])
            near = jnp.where(away == k, value, near)
            far = jnp.where((ahead == k) & crosses, value, far)
        band[...] = near.astype(jnp.bfloat16)
        corner[...] = far.astype(jnp.bfloat16)

    def times(values, weights):
        head = values.astype(jnp.bfloat16)
        rest = (values - head.astype(jnp.float32)).astype(jnp.bfloat16)
        both = jnp.dot(
            jnp.concatenate([head, rest], axis=1), weights[...], preferred_element_type=jnp.float32
        )
        return both[:, :COLS] + both[:, COLS:]

    def block(b):
        return pl.ds(pl.multiple_of(b * 8, 8), 8)

    def inner(b, shift=0):
        return pl.ds(pl.multiple_of(b * 8, 8) + (8 + shift), 8)

    def pack_x(field):
        for f in range(4):
            for lev in range(LEVELS):
                x_send[0, f * 8 + lev] = field[f, lev, 8:12, :]
                x_send[1, f * 8 + lev] = field[f, lev, ROWS + 4 : ROWS + 8, :]

    def pack_y(field):
        def body(b, carry):
            packed = []
            for pair in range(2):
                total = jnp.zeros((8, COLS), jnp.float32)
                for i in range(16):
                    value = field[2 * pair + i // 8, i % 8, inner(b), :]
                    rolled = pltpu.roll(value, (8 * i + 4) % COLS, 1)
                    total = jnp.where(group == i, rolled, total)
                packed.append(total)
            y_send[0, block(b), :] = jnp.where(low_half, packed[0], pltpu.roll(packed[1], 4, 1))
            y_send[1, block(b), :] = jnp.where(low_half, pltpu.roll(packed[0], COLS - 4, 1), packed[1])
            return carry

        lax.fori_loop(0, BLOCKS, body, 0)

    def halo_copies(turn):
        return [
            remote(x_send.at[0], x_recv.at[turn, 0], x_sems.at[0, turn, 0], x_sems.at[1, turn, 0], x_id(-1)),
            remote(x_send.at[1], x_recv.at[turn, 1], x_sems.at[0, turn, 1], x_sems.at[1, turn, 1], x_id(1)),
            remote(y_send.at[0], y_recv.at[turn, 0], y_sems.at[0, turn, 0], y_sems.at[1, turn, 0], y_id(1)),
            remote(y_send.at[1], y_recv.at[turn, 1], y_sems.at[0, turn, 1], y_sems.at[1, turn, 1], y_id(-1)),
        ]

    def inside(field):
        def along_y(f, carry):
            values = field[f, :, 8 : 8 + ROWS, :].reshape(LEVELS * ROWS, COLS)
            lap[f] = times(values, band).reshape(LEVELS, ROWS, COLS)
            return carry

        lax.fori_loop(0, 4, along_y, 0)

        def along_xz(b, carry):
            for f in range(4):
                centre = [field[f, lev, inner(b), :] for lev in range(LEVELS)]
                for lev in range(LEVELS):
                    total = lap[f, lev, block(b), :] + (3.0 * COEFS[0]) * centre[lev]
                    for k in range(1, 5):
                        near = field[f, lev, inner(b, k), :] + field[f, lev, inner(b, -k), :]
                        if lev + k < LEVELS:
                            near += centre[lev + k]
                        if lev - k >= 0:
                            near += centre[lev - k]
                        total += COEFS[k] * near
                    lap[f, lev, block(b), :] = total
            return carry

        lax.fori_loop(0, BLOCKS, along_xz, 0)

    def unpack_y(turn):
        tails = jnp.where(gy == 0, 0.0, y_recv[turn, 0])
        heads = jnp.where(gy == n_y - 1, 0.0, y_recv[turn, 1])
        low = (lax.broadcasted_iota(jnp.int32, (ROWS, COLS), 1) & 4) == 0
        first = jnp.where(low, heads, pltpu.roll(tails, COLS - 4, 1))
        second = jnp.where(low, pltpu.roll(heads, COLS - 4, 1), pltpu.roll(tails, COLS - 8, 1))
        sides[...] = times(jnp.concatenate([first, second], axis=0), corner).reshape(2, ROWS, COLS)

    def unpack_x(turn):
        def body(f, carry):
            for lev in range(LEVELS):
                i = f * LEVELS + lev
                edge[0, i, 4:8, :] = jnp.where(gx == 0, 0.0, x_recv[turn, 1, i])
                edge[1, i, 8:12, :] = jnp.where(gx == n_x - 1, 0.0, x_recv[turn, 0, i])
            for lev in range(LEVELS):
                i = f * LEVELS + lev
                top = lap[f, lev, 0:8, :]
                bottom = lap[f, lev, ROWS - 8 : ROWS, :]
                for k in range(1, 5):
                    top += COEFS[k] * edge[0, i, 8 - k : 16 - k, :]
                    bottom += COEFS[k] * edge[1, i, k : k + 8, :]
                lap[f, lev, 0:8, :] = top
                lap[f, lev, ROWS - 8 : ROWS, :] = bottom
            return carry

        lax.fori_loop(0, 4, body, 0)

    outer = (lane < 4) | (lane >= COLS - 4)

    def laplace(f, b):
        side = sides[f // 2, block(b), :]
        results = []
        for lev in range(LEVELS):
            at = (8 * (f % 2) + lev) * 8
            turned = pltpu.roll(side, COLS - at, 1) if at else side
            results.append(lap[f, lev, block(b), :] + jnp.where(outer, turned, 0.0))
        return results

    def old(turn, f, lev, b):
        return prev[f, lev, block(b), :] if turn == 0 else field0[f, lev, inner(b), :]

    def put(turn, f, lev, b, value):
        if turn == 0:
            field1[f, lev, inner(b), :] = value
        else:
            prev[f, lev, block(b), :] = value

    def incident(turn, field):
        def body(b, curv):
            u = [field[0, lev, inner(b), :] for lev in range(LEVELS)]
            du = [field[1, lev, inner(b), :] for lev in range(LEVELS)]
            lap_u = laplace(0, b)
            lap_du = laplace(1, b)
            inv = planes[0, block(b), :]
            fade = planes[1, block(b), :]
            for lev in range(LEVELS):
                lam = field[2, lev, inner(b), :]
                dlam = field[3, lev, inner(b), :]
                grad = lam * lap_u[lev]
                hess = dlam * lap_u[lev] + lam * lap_du[lev]
                if turn == 1:
                    grad += terms[0, lev, block(b), :]
                    hess += terms[1, lev, block(b), :]
                terms[0, lev, block(b), :] = grad
                terms[1, lev, block(b), :] = hess
                direction = born[lev, block(b), :]
                if turn == 1:
                    curv += direction * hess
                pace = speed[lev, block(b), :]
                new_u = 2.0 * u[lev] + pace * lap_u[lev]
                if lev == 1:
                    new_u += planes[2 + turn, block(b), :]
                new_du = 2.0 * du[lev] + pace * lap_du[lev] + direction * lap_u[lev]
                put(turn, 0, lev, b, new_u * inv - fade * old(turn, 0, lev, b))
                put(turn, 1, lev, b, new_du * inv - fade * old(turn, 1, lev, b))
            return curv

        return lax.fori_loop(0, BLOCKS, body, jnp.zeros((8, COLS), jnp.float32))

    def adjoint(turn, field):
        def body(b, carry):
            lam = [field[2, lev, inner(b), :] for lev in range(LEVELS)]
            dlam = [field[3, lev, inner(b), :] for lev in range(LEVELS)]
            lap_lam = laplace(2, b)
            lap_dlam = laplace(3, b)
            inv = planes[0, block(b), :]
            fade = planes[1, block(b), :]
            for lev in range(LEVELS):
                pace = speed[lev, block(b), :]
                new_lam = 2.0 * lam[lev] + pace * lap_lam[lev]
                new_dlam = 2.0 * dlam[lev] + pace * lap_dlam[lev] + born[lev, block(b), :] * lap_lam[lev]
                if lev == 1:
                    new_lam += planes[4 + turn, block(b), :]
                    new_dlam += planes[6, block(b), :] * field[1, lev, inner(b), :]
                put(turn, 2, lev, b, new_lam * inv - fade * old(turn, 2, lev, b))
                put(turn, 3, lev, b, new_dlam * inv - fade * old(turn, 3, lev, b))
            return carry

        lax.fori_loop(0, BLOCKS, body, 0)

    def step_halos(field, turn, greet):
        pack_x(field)
        if greet:
            pl.semaphore_wait(barrier, len(partners))
        copies = halo_copies(turn)
        for copy in copies[:2]:
            copy.start()
        pack_y(field)
        for copy in copies[2:]:
            copy.start()
        return copies

    for field in (field0, field1):
        for f in range(4):
            for lev in range(LEVELS):
                field[f, lev, 0:8, :] = jnp.zeros((8, COLS), jnp.float32)
                field[f, lev, ROWS + 8 : ROWS + 16, :] = jnp.zeros((8, COLS), jnp.float32)
    for i in range(32):
        edge[0, i, 0:8, :] = jnp.zeros((8, COLS), jnp.float32)
        edge[0, i, 8:16, :] = jnp.zeros((8, COLS), jnp.float32)
        edge[1, i, 0:8, :] = jnp.zeros((8, COLS), jnp.float32)
        edge[1, i, 8:16, :] = jnp.zeros((8, COLS), jnp.float32)
    loads[0].wait()
    copies = step_halos(field0, 0, True)
    build_weights()
    build_planes()
    inside(field0)
    for load in loads[1:]:
        load.wait()
    for copy in copies[2:]:
        copy.wait()
    unpack_y(0)
    for copy in copies[:2]:
        copy.wait()
    unpack_x(0)
    incident(0, field0)
    adjoint(0, field0)

    copies = step_halos(field1, 1, False)
    inside(field1)
    for copy in copies[2:]:
        copy.wait()
    unpack_y(1)
    for copy in copies[:2]:
        copy.wait()
    unpack_x(1)
    curv = incident(1, field1)

    swap = remote(terms.at[1 - core], sib, sib_sems.at[0], sib_sems.at[1], sib_id)
    swap.start()
    curv_sib[core] = curv
    curv_swap = remote(curv_sib.at[core], curv_sib.at[core], cs_sems.at[0], cs_sems.at[1], sib_id)
    curv_swap.start()
    adjoint(1, field1)
    save = pltpu.make_async_copy(prev, out_ref.at[0], out_sem)
    save.start()

    def spread(buffer, place, value, sems, ident, count):
        buffer[place] = value
        sent = [
            remote(buffer.at[place], buffer.at[place], sems.at[0, k - 1], sems.at[1, k - 1], ident(k))
            for k in range(1, count)
        ]
        for copy in sent:
            copy.start()
        return sent

    def gather(sent, buffer, count):
        for copy in sent:
            copy.wait()
        total = buffer[0]
        for k in range(1, count):
            total = total + buffer[k]
        return total

    def owner(k):
        return pl.ds(lax.rem(z + k + 2 * n_z, n_z) * per, per)

    halves = (pl.ds(0, ROWS // 2), pl.ds(ROWS // 2, ROWS // 2))
    full = pl.ds(0, ROWS)
    signs = (1, -1)

    def add(level, rows, *others):
        total = terms[core, level, rows, :]
        for other in others:
            total = total + other
        terms[core, level, rows, :] = total

    def share(way, k):
        copy = remote(
            terms.at[core, owner(signs[way] * k), full, :],
            direct.at[way, k - 1],
            rs_sems.at[0, way, k],
            rs_sems.at[1, way, k],
            z_id(signs[way] * k),
        )
        copy.start()
        return copy

    swap.wait()
    joins = []
    for way in range(2):
        level = owner(reach)
        rows = halves[way]
        add(level, rows, sib[level, rows, :])
        copy = remote(
            terms.at[core, level, rows, :],
            join.at[way, :, rows, :],
            rs_sems.at[0, way, 0],
            rs_sems.at[1, way, 0],
            z_id(signs[way]),
        )
        copy.start()
        joins.append(copy)
    shares = []
    for k in range(reach - 2, 0, -1):
        for way in range(2):
            level = owner(signs[way] * k)
            add(level, full, sib[level, full, :])
            shares.append(share(way, k))
    curv_swap.wait()
    curv = curv_sib[0] + curv_sib[1]
    sent_y = spread(curv_x, gx, curv, cx_sems, x_id, n_x)
    for way in range(2):
        level = owner(signs[way] * (reach - 1))
        add(level, full, sib[level, full, :])
    add(owner(0), full, sib[owner(0), full, :])
    for way in range(2):
        joins[way].wait_recv()
        level = owner(signs[way] * (reach - 1))
        add(level, halves[way], join[way, :, halves[way], :])
        shares.append(share(way, reach - 1))
    curv = gather(sent_y, curv_x, n_x)
    sent_x = spread(curv_y, gy, curv, cy_sems, y_id, n_y)
    for copy in shares:
        copy.wait_recv()
    total = terms[core, owner(0)]
    for way in range(2):
        for k in range(1, reach):
            total = total + direct[way, k - 1]
    sums_ref[core, owner(0)] = total * (1.0 / shots)

    def pass_on(level, rows, pair, who):
        copy = remote(
            sums_ref.at[core, level, rows, :],
            sums_ref.at[core, level, rows, :],
            pair.at[0],
            pair.at[1],
            who,
        )
        copy.start()
        return copy

    spreads = {}
    for k in range(reach - 1, 0, -1):
        for way in range(2):
            spreads[way, k] = pass_on(
                owner(0), full, ag_sems.at[way, k - 1], z_id(signs[way] * k)
            )
    across = [pass_on(owner(0), full, agsib_sems.at[0], sib_id)]
    for copy in joins + shares:
        copy.wait_send()
    curv = gather(sent_x, curv_y, n_y)
    sent_z = spread(curv_z, z, curv, cz_sems, z_id, n_z)
    lasts = []
    for k in range(1, reach):
        for way in range(2):
            spreads[way, k].wait_recv()
            level = owner(-signs[way] * k)
            if k == reach - 1:
                lasts.append(pass_on(level, halves[way], last_sems.at[way, 0], z_id(signs[way])))
                lasts.append(pass_on(level, halves[way], last_sems.at[way, 1], cross_id(signs[way])))
            across.append(pass_on(level, full, agsib_sems.at[2 * k - 1 + way], sib_id))
    curv = gather(sent_z, curv_z, n_z)
    cells = LEVELS * whole_x * whole_y
    curv_ref[0, 0] = jnp.sum(curv) * (1.0 / (shots * math.sqrt(cells)))
    for copy in spreads.values():
        copy.wait_send()
    save.wait()
    for copy in across + lasts:
        copy.wait()


def local(sizes, *args):
    shots, n_x, n_y = sizes
    n_z = shots // 2
    reach = n_z // 2
    per = LEVELS // n_z
    any_space = pl.BlockSpec(memory_space=pl.ANY)
    smem = pl.BlockSpec(memory_space=pltpu.SMEM)
    vmem = pl.BlockSpec(memory_space=pltpu.VMEM)
    f32 = jnp.float32
    dma = pltpu.SemaphoreType.DMA
    tile = (8, COLS)
    fields, sums, curv = pl.pallas_call(
        functools.partial(kernel, sizes),
        out_shape=(
            jax.ShapeDtypeStruct((1, 4, LEVELS, ROWS, COLS), f32),
            jax.ShapeDtypeStruct((2, LEVELS, ROWS, COLS), f32),
            jax.ShapeDtypeStruct((1, 1), f32),
        ),
        in_specs=[any_space] * 12,
        out_specs=(any_space, vmem, smem),
        scratch_shapes=[
            pltpu.VMEM((4, LEVELS, ROWS + 16, COLS), f32),
            pltpu.VMEM((4, LEVELS, ROWS + 16, COLS), f32),
            pltpu.VMEM((4, LEVELS, ROWS, COLS), f32),
            pltpu.VMEM((LEVELS, ROWS, COLS), f32),
            pltpu.VMEM((LEVELS, ROWS, COLS), f32),
            pltpu.VMEM((2, LEVELS, ROWS, COLS), f32),
            pltpu.VMEM((LEVELS, ROWS, COLS), f32),
            pltpu.VMEM((4, LEVELS, ROWS, COLS), f32),
            pltpu.VMEM((2 * COLS, 2 * COLS), jnp.bfloat16),
            pltpu.VMEM((2 * COLS, 2 * COLS), jnp.bfloat16),
            pltpu.VMEM((2, per, ROWS, COLS), f32),
            pltpu.VMEM((2, reach - 1, per, ROWS, COLS), f32),
            pltpu.VMEM((2, 32, 4, COLS), f32),
            pltpu.VMEM((2, 2, 32, 4, COLS), f32),
            pltpu.VMEM((2, ROWS, COLS), f32),
            pltpu.VMEM((2, 2, ROWS, COLS), f32),
            pltpu.VMEM((2, 32, 16, COLS), f32),
            pltpu.VMEM((2, ROWS, COLS), f32),
            pltpu.VMEM((7, ROWS, COLS), f32),
            pltpu.VMEM((2,) + tile, f32),
            pltpu.VMEM((n_y,) + tile, f32),
            pltpu.VMEM((n_x,) + tile, f32),
            pltpu.VMEM((n_z,) + tile, f32),
            pltpu.SMEM(args[4].shape, jnp.int32),
            pltpu.SMEM(args[5].shape, jnp.int32),
            pltpu.SMEM(args[6].shape, jnp.int32),
            pltpu.SMEM(args[7].shape, jnp.int32),
            pltpu.SMEM(args[8].shape, f32),
            pltpu.VMEM(args[9].shape, jnp.int32),
            pltpu.VMEM(args[10].shape, jnp.int32),
            pltpu.VMEM(args[11].shape, f32),
            dma((4,)),
            dma((8,)),
            dma((2, 2, 2)),
            dma((2, 2, 2)),
            dma,
            dma((2,)),
            dma((2, 2, reach)),
            dma((2, reach - 1, 2)),
            dma((2 * reach - 1, 2)),
            dma((2, 2, 2)),
            dma((2,)),
            dma((2, n_y - 1)),
            dma((2, n_x - 1)),
            dma((2, n_z - 1)),
        ],
        compiler_params=pltpu.CompilerParams(
            collective_id=0, has_side_effects=True, vmem_limit_bytes=60 * 1024 * 1024
        ),
    )(*args)
    return fields, sums[0], sums[1], curv[0, 0]


def solution(mesh):
    sizes = (mesh.shape["shot"], mesh.shape["gx"], mesh.shape["gy"])
    placed = (
        P("shot", None, None, "gx", "gy"),
        P("shot", None, None, "gx", "gy"),
        P(None, "gx", "gy"),
        P(None, "gx", "gy"),
        P(),
        P(),
        P("shot"),
        P("shot"),
        P("shot", None),
        P("shot", None),
        P("shot", None),
        P("shot", None, None),
    )
    return jax.shard_map(
        functools.partial(local, sizes),
        mesh=mesh,
        in_specs=placed,
        out_specs=(
            P("shot", None, None, "gx", "gy"),
            P(None, "gx", "gy"),
            P(None, "gx", "gy"),
            P(),
        ),
        check_vma=False,
    )
```

time: 77.2 us -> 55.1 us (0.71)
  Pallas kernels: 64.1 us -> 48.3 us
  local copies, waits for them, and re-layouts: 8.88 us -> 2.93 us
    pallas_call x1, Pallas kernels: 64.1 us -> 48.3 us  [local(): pl.pallas_call(functools.partial(kernel, sizes), out_shape=(jax.ShapeDtyp...]
    unnamed x21 -> x3, local copies, waits for them, and re-layouts: 8.05 us -> 0.97 us
    squeeze x1, local copies, waits for them, and re-layouts: 0.83 us -> 1.96 us  [local(): return (fields, sums[0], sums[1], curv[0, 0])]
where the time goes in v2:
time: 55.1 us; the launch traced here: 54.9 us
  Pallas kernels  48.3 us (88%)
  between operations  3.7 us (7%)
  local copies, waits for them, and re-layouts  2.93 us (5%)
    pallas_call x1, Pallas kernels, local(): pl.pallas_call(functools.partial(kernel, sizes), out_shape=(jax.ShapeDtyp...  48.3 us
    squeeze x1, local copies, waits for them, and re-layouts, local(): return (fields, sums[0], sums[1], curv[0, 0])  1.96 us

profile of v2, /device:TPU:1, one launch (start us, length us, event | category | flops | bytes accessed | tf_op | source)
XLA Modules:
  0.0 54.9 jit_solution(9245151051398226841)
XLA Ops:
  1.9 48.3 %shard_map.147 = (f32[1,4,8,64,128]{4,3,2,1,0:T(8,128)}, f32[2,8,64,128]{3,2,1,0:T(8,128)}, f32[1,1]{1,0:T(1,128)}) custom-call(f32[1,4,8,64,128]{4,3,2,1,0:T(8,128)} %now_ref.1, f32[1,4,8,64,128]{4,3,2,1,0:T(8,128)} %before_ref.1, f32[8,64,128]{2,1,0:T(8,128)} %speed_ref.1, f32[8,64,128]{2,1,0:T(8,128)} %born_ref.1, s32[512]{0:T(512)} %pml_x_ref.1, ...), custom_call_target="tpu_custom_call" | custom-call | tf_op jit(solution)/shard_map/pallas_call | solution.py:586
  50.2 0.0 copy-start
  50.3 2.0 %slice_bitcast_fusion = (f32[8,64,128]{2,1,0:T(8,128)}, f32[8,64,128]{2,1,0:T(8,128)}) fusion(f32[2,8,64,128]{3,2,1,0:T(8,128)} %get-tuple-element.8), kind=kLoop, calls=%fused_computation | loop fusion | bytes 1048576 | tf_op jit(solution)/shard_map/squeeze | solution.py:646
  52.2 0.0 copy-done
  52.2 1.0 %copy.20 = f32[1,4,8,64,128]{4,3,2,1,0:T(8,128)} copy(f32[1,4,8,64,128]{4,3,2,1,0:T(8,128)S(1)} %copy-done) | data formatting | bytes 2097152
Async XLA Ops:
  50.2 2.0 %copy-start = (f32[1,4,8,64,128]{4,3,2,1,0:T(8,128)S(1)}, f32[1,4,8,64,128]{4,3,2,1,0:T(8,128)}, u32[]{:S(2)}) copy-start(f32[1,4,8,64,128]{4,3,2,1,0:T(8,128)} %get-tuple-element.16) | copy-start | bytes 3145732

commit v3 on v2

--- a/solution.py
+++ b/solution.py
@@ -60,6 +60,7 @@
     x_recv,
     y_send,
     y_recv,
+    packed,
     edge,
     sides,
     planes,
@@ -79,7 +80,6 @@
     small_sems,
     x_sems,
     y_sems,
-    out_sem,
     sib_sems,
     rs_sems,
     ag_sems,
@@ -120,10 +120,16 @@
         )
 
     loads = [
-        pltpu.make_async_copy(now_ref.at[0], field0.at[:, :, pl.ds(8, ROWS), :], in_sems.at[0]),
-        pltpu.make_async_copy(before_ref.at[0], prev, in_sems.at[1]),
-        pltpu.make_async_copy(speed_ref, speed, in_sems.at[2]),
-        pltpu.make_async_copy(born_ref, born, in_sems.at[3]),
+        pltpu.make_async_copy(
+            now_ref.at[0, pl.ds(2 * pair, 2)],
+            field0.at[pl.ds(2 * pair, 2), :, pl.ds(8, ROWS), :],
+            in_sems.at[pair],
+        )
+        for pair in range(2)
+    ] + [
+        pltpu.make_async_copy(before_ref.at[0], prev, in_sems.at[2]),
+        pltpu.make_async_copy(speed_ref, speed, in_sems.at[3]),
+        pltpu.make_async_copy(born_ref, born, in_sems.at[4]),
     ]
     small = [
         pltpu.make_async_copy(source, target, small_sems.at[i])
@@ -140,7 +146,7 @@
             ]
         )
     ]
-    for load in [loads[0]] + small + loads[1:]:
+    for load in loads[:2] + small + loads[2:]:
         load.start()
 
     barrier = pltpu.get_barrier_semaphore()
@@ -197,8 +203,7 @@
         planes[6] = parts[0]
 
     lane = lax.broadcasted_iota(jnp.int32, (8, COLS), 1)
-    low_half = (lane & 4) == 0
-    group = lane // 8
+    group = ((lane + 4) & (COLS - 1)) // 8
 
     def build_weights():
         shape = (2 * COLS, 2 * COLS)
@@ -234,46 +239,67 @@
     def inner(b, shift=0):
         return pl.ds(pl.multiple_of(b * 8, 8) + (8 + shift), 8)
 
-    def pack_x(field):
-        for f in range(4):
-            for lev in range(LEVELS):
-                x_send[0, f * 8 + lev] = field[f, lev, 8:12, :]
-                x_send[1, f * 8 + lev] = field[f, lev, ROWS + 4 : ROWS + 8, :]
-
-    def pack_y(field):
+    def pack_x(field, turn, pair):
+        for i in range(16):
+            f, lev = 2 * pair + i // LEVELS, i % LEVELS
+            x_send[turn, pair, 0, i] = field[f, lev, 8:12, :]
+            x_send[turn, pair, 1, i] = field[f, lev, ROWS + 4 : ROWS + 8, :]
+
+    def borders(values):
+        total = values[0]
+        for i in range(1, 16):
+            total = jnp.where(group == i, pltpu.roll(values[i], 8 * i, 1), total)
+        return total
+
+    def pack_y(field, pair):
         def body(b, carry):
-            packed = []
-            for pair in range(2):
-                total = jnp.zeros((8, COLS), jnp.float32)
-                for i in range(16):
-                    value = field[2 * pair + i // 8, i % 8, inner(b), :]
-                    rolled = pltpu.roll(value, (8 * i + 4) % COLS, 1)
-                    total = jnp.where(group == i, rolled, total)
-                packed.append(total)
-            y_send[0, block(b), :] = jnp.where(low_half, packed[0], pltpu.roll(packed[1], 4, 1))
-            y_send[1, block(b), :] = jnp.where(low_half, pltpu.roll(packed[0], COLS - 4, 1), packed[1])
+            values = [field[2 * pair + i // LEVELS, i % LEVELS, inner(b), :] for i in range(16)]
+            packed[pair, block(b), :] = borders(values)
             return carry
 
         lax.fori_loop(0, BLOCKS, body, 0)
 
-    def halo_copies(turn):
-        return [
-            remote(x_send.at[0], x_recv.at[turn, 0], x_sems.at[0, turn, 0], x_sems.at[1, turn, 0], x_id(-1)),
-            remote(x_send.at[1], x_recv.at[turn, 1], x_sems.at[0, turn, 1], x_sems.at[1, turn, 1], x_id(1)),
-            remote(y_send.at[0], y_recv.at[turn, 0], y_sems.at[0, turn, 0], y_sems.at[1, turn, 0], y_id(1)),
-            remote(y_send.at[1], y_recv.at[turn, 1], y_sems.at[0, turn, 1], y_sems.at[1, turn, 1], y_id(-1)),
+    half_rows = ROWS // 2
+    is_tail = (lax.broadcasted_iota(jnp.int32, (half_rows, COLS), 1) & 4) != 0
+
+    def fold_y(turn, pair):
+        first = packed[pair, 0:half_rows, :]
+        second = packed[pair, half_rows:ROWS, :]
+        y_send[turn, pair, 0] = jnp.where(is_tail, first, pltpu.roll(second, 4, 1))
+        y_send[turn, pair, 1] = jnp.where(is_tail, pltpu.roll(second, COLS - 4, 1), first)
+
+    def halos(buffer_out, buffer_in, sems, turn, pair, ident, ways):
+        copies = [
+            remote(
+                buffer_out.at[turn, pair, way],
+                buffer_in.at[turn, pair, way],
+                sems.at[0, turn, pair, way],
+                sems.at[1, turn, pair, way],
+                ident(ways[way]),
+            )
+            for way in range(2)
         ]
-
-    def inside(field):
+        for copy in copies:
+            copy.start()
+        return copies
+
+    def send_x(turn, pair):
+        return halos(x_send, x_recv, x_sems, turn, pair, x_id, (-1, 1))
+
+    def send_y(turn, pair):
+        fold_y(turn, pair)
+        return halos(y_send, y_recv, y_sems, turn, pair, y_id, (1, -1))
+
+    def inside(field, pair):
         def along_y(f, carry):
             values = field[f, :, 8 : 8 + ROWS, :].reshape(LEVELS * ROWS, COLS)
             lap[f] = times(values, band).reshape(LEVELS, ROWS, COLS)
             return carry
 
-        lax.fori_loop(0, 4, along_y, 0)
+        lax.fori_loop(2 * pair, 2 * pair + 2, along_y, 0)
 
         def along_xz(b, carry):
-            for f in range(4):
+            for f in (2 * pair, 2 * pair + 1):
                 centre = [field[f, lev, inner(b), :] for lev in range(LEVELS)]
                 for lev in range(LEVELS):
                     total = lap[f, lev, block(b), :] + (3.0 * COEFS[0]) * centre[lev]
@@ -289,20 +315,20 @@
 
         lax.fori_loop(0, BLOCKS, along_xz, 0)
 
-    def unpack_y(turn):
-        tails = jnp.where(gy == 0, 0.0, y_recv[turn, 0])
-        heads = jnp.where(gy == n_y - 1, 0.0, y_recv[turn, 1])
-        low = (lax.broadcasted_iota(jnp.int32, (ROWS, COLS), 1) & 4) == 0
-        first = jnp.where(low, heads, pltpu.roll(tails, COLS - 4, 1))
-        second = jnp.where(low, pltpu.roll(heads, COLS - 4, 1), pltpu.roll(tails, COLS - 8, 1))
-        sides[...] = times(jnp.concatenate([first, second], axis=0), corner).reshape(2, ROWS, COLS)
-
-    def unpack_x(turn):
+    def unpack_y(turn, pair):
+        tails = jnp.where(gy == 0, 0.0, y_recv[turn, pair, 0])
+        heads = jnp.where(gy == n_y - 1, 0.0, y_recv[turn, pair, 1])
+        first = jnp.where(is_tail, tails, heads)
+        second = jnp.where(is_tail, pltpu.roll(tails, COLS - 4, 1), pltpu.roll(heads, 4, 1))
+        sides[pair] = times(jnp.concatenate([first, second], axis=0), corner)
+
+    def unpack_x(turn, pair):
         def body(f, carry):
             for lev in range(LEVELS):
                 i = f * LEVELS + lev
-                edge[0, i, 4:8, :] = jnp.where(gx == 0, 0.0, x_recv[turn, 1, i])
-                edge[1, i, 8:12, :] = jnp.where(gx == n_x - 1, 0.0, x_recv[turn, 0, i])
+                mine = (f - 2 * pair) * LEVELS + lev
+                edge[0, i, 4:8, :] = jnp.where(gx == 0, 0.0, x_recv[turn, pair, 1, mine])
+                edge[1, i, 8:12, :] = jnp.where(gx == n_x - 1, 0.0, x_recv[turn, pair, 0, mine])
             for lev in range(LEVELS):
                 i = f * LEVELS + lev
                 top = lap[f, lev, 0:8, :]
@@ -314,7 +340,7 @@
                 lap[f, lev, ROWS - 8 : ROWS, :] = bottom
             return carry
 
-        lax.fori_loop(0, 4, body, 0)
+        lax.fori_loop(2 * pair, 2 * pair + 2, body, 0)
 
     outer = (lane < 4) | (lane >= COLS - 4)
 
@@ -330,11 +356,15 @@
     def old(turn, f, lev, b):
         return prev[f, lev, block(b), :] if turn == 0 else field0[f, lev, inner(b), :]
 
-    def put(turn, f, lev, b, value):
+    def finish(turn, pair, b, fresh):
+        for i in range(16):
+            f, lev = 2 * pair + i // LEVELS, i % LEVELS
+            if turn == 0:
+                field1[f, lev, inner(b), :] = fresh[i]
+            else:
+                out_ref[0, f, lev, block(b), :] = fresh[i]
         if turn == 0:
-            field1[f, lev, inner(b), :] = value
-        else:
-            prev[f, lev, block(b), :] = value
+            packed[pair, block(b), :] = borders(fresh)
 
     def incident(turn, field):
         def body(b, curv):
@@ -342,6 +372,7 @@
             du = [field[1, lev, inner(b), :] for lev in range(LEVELS)]
             lap_u = laplace(0, b)
             lap_du = laplace(1, b)
+            fresh = [None] * 16
             inv = planes[0, block(b), :]
             fade = planes[1, block(b), :]
             for lev in range(LEVELS):
@@ -362,8 +393,9 @@
                 if lev == 1:
                     new_u += planes[2 + turn, block(b), :]
                 new_du = 2.0 * du[lev] + pace * lap_du[lev] + direction * lap_u[lev]
-                put(turn, 0, lev, b, new_u * inv - fade * old(turn, 0, lev, b))
-                put(turn, 1, lev, b, new_du * inv - fade * old(turn, 1, lev, b))
+                fresh[lev] = new_u * inv - fade * old(turn, 0, lev, b)
+                fresh[LEVELS + lev] = new_du * inv - fade * old(turn, 1, lev, b)
+            finish(turn, 0, b, fresh)
             return curv
 
         return lax.fori_loop(0, BLOCKS, body, jnp.zeros((8, COLS), jnp.float32))
@@ -374,6 +406,7 @@
             dlam = [field[3, lev, inner(b), :] for lev in range(LEVELS)]
             lap_lam = laplace(2, b)
             lap_dlam = laplace(3, b)
+            fresh = [None] * 16
             inv = planes[0, block(b), :]
             fade = planes[1, block(b), :]
             for lev in range(LEVELS):
@@ -383,23 +416,12 @@
                 if lev == 1:
                     new_lam += planes[4 + turn, block(b), :]
                     new_dlam += planes[6, block(b), :] * field[1, lev, inner(b), :]
-                put(turn, 2, lev, b, new_lam * inv - fade * old(turn, 2, lev, b))
-                put(turn, 3, lev, b, new_dlam * inv - fade * old(turn, 3, lev, b))
+                fresh[lev] = new_lam * inv - fade * old(turn, 2, lev, b)
+                fresh[LEVELS + lev] = new_dlam * inv - fade * old(turn, 3, lev, b)
+            finish(turn, 1, b, fresh)
             return carry
 
         lax.fori_loop(0, BLOCKS, body, 0)
-
-    def step_halos(field, turn, greet):
-        pack_x(field)
-        if greet:
-            pl.semaphore_wait(barrier, len(partners))
-        copies = halo_copies(turn)
-        for copy in copies[:2]:
-            copy.start()
-        pack_y(field)
-        for copy in copies[2:]:
-            copy.start()
-        return copies
 
     for field in (field0, field1):
         for f in range(4):
@@ -411,30 +433,45 @@
         edge[0, i, 8:16, :] = jnp.zeros((8, COLS), jnp.float32)
         edge[1, i, 0:8, :] = jnp.zeros((8, COLS), jnp.float32)
         edge[1, i, 8:16, :] = jnp.zeros((8, COLS), jnp.float32)
-    loads[0].wait()
-    copies = step_halos(field0, 0, True)
+    x_copies = {}
+    y_copies = {}
+    for pair in range(2):
+        loads[pair].wait()
+        pack_x(field0, 0, pair)
+        if pair == 0:
+            pl.semaphore_wait(barrier, len(partners))
+        x_copies[0, pair] = send_x(0, pair)
+        pack_y(field0, pair)
+        y_copies[0, pair] = send_y(0, pair)
     build_weights()
     build_planes()
-    inside(field0)
-    for load in loads[1:]:
+    inside(field0, 0)
+    inside(field0, 1)
+    for load in loads[2:]:
         load.wait()
-    for copy in copies[2:]:
-        copy.wait()
-    unpack_y(0)
-    for copy in copies[:2]:
-        copy.wait()
-    unpack_x(0)
+
+    def take(turn, pair):
+        for copy in y_copies[turn, pair]:
+            copy.wait_recv()
+        unpack_y(turn, pair)
+        for copy in x_copies[turn, pair]:
+            copy.wait_recv()
+        unpack_x(turn, pair)
+
+    take(0, 0)
     incident(0, field0)
+    pack_x(field1, 1, 0)
+    x_copies[1, 0] = send_x(1, 0)
+    y_copies[1, 0] = send_y(1, 0)
+    take(0, 1)
     adjoint(0, field0)
-
-    copies = step_halos(field1, 1, False)
-    inside(field1)
-    for copy in copies[2:]:
-        copy.wait()
-    unpack_y(1)
-    for copy in copies[:2]:
-        copy.wait()
-    unpack_x(1)
+    pack_x(field1, 1, 1)
+    x_copies[1, 1] = send_x(1, 1)
+    y_copies[1, 1] = send_y(1, 1)
+
+    inside(field1, 0)
+    inside(field1, 1)
+    take(1, 0)
     curv = incident(1, field1)
 
     swap = remote(terms.at[1 - core], sib, sib_sems.at[0], sib_sems.at[1], sib_id)
@@ -442,9 +479,11 @@
     curv_sib[core] = curv
     curv_swap = remote(curv_sib.at[core], curv_sib.at[core], cs_sems.at[0], cs_sems.at[1], sib_id)
     curv_swap.start()
+    take(1, 1)
     adjoint(1, field1)
-    save = pltpu.make_async_copy(prev, out_ref.at[0], out_sem)
-    save.start()
+    for copies in list(x_copies.values()) + list(y_copies.values()):
+        for copy in copies:
+            copy.wait_send()
 
     def spread(buffer, place, value, sems, ident, count):
         buffer[place] = value
@@ -564,11 +603,28 @@
             across.append(pass_on(level, full, agsib_sems.at[2 * k - 1 + way], sib_id))
     curv = gather(sent_z, curv_z, n_z)
     cells = LEVELS * whole_x * whole_y
-    curv_ref[0, 0] = jnp.sum(curv) * (1.0 / (shots * math.sqrt(cells)))
+    curv_ref[...] = jnp.sum(curv, keepdims=True) * (1.0 / (shots * math.sqrt(cells)))
     for copy in spreads.values():
         copy.wait_send()
-    save.wait()
     for copy in across + lasts:
+        copy.wait()
+
+
+def deliver(fields_ref, sums_ref, curv_ref, out_ref, grad_ref, hess_ref, total_ref, sems):
+    copies = [
+        pltpu.make_async_copy(source, target, sems.at[i])
+        for i, (source, target) in enumerate(
+            [
+                (fields_ref, out_ref),
+                (sums_ref.at[0], grad_ref),
+                (sums_ref.at[1], hess_ref),
+                (curv_ref, total_ref),
+            ]
+        )
+    ]
+    for copy in copies:
+        copy.start()
+    for copy in copies:
         copy.wait()
 
 
@@ -578,7 +634,7 @@
     reach = n_z // 2
     per = LEVELS // n_z
     any_space = pl.BlockSpec(memory_space=pl.ANY)
-    smem = pl.BlockSpec(memory_space=pltpu.SMEM)
+    hbm = pl.BlockSpec(memory_space=pltpu.HBM)
     vmem = pl.BlockSpec(memory_space=pltpu.VMEM)
     f32 = jnp.float32
     dma = pltpu.SemaphoreType.DMA
@@ -586,12 +642,12 @@
     fields, sums, curv = pl.pallas_call(
         functools.partial(kernel, sizes),
         out_shape=(
-            jax.ShapeDtypeStruct((1, 4, LEVELS, ROWS, COLS), f32),
-            jax.ShapeDtypeStruct((2, LEVELS, ROWS, COLS), f32),
-            jax.ShapeDtypeStruct((1, 1), f32),
+            pltpu.VMEM((1, 4, LEVELS, ROWS, COLS), f32),
+            pltpu.VMEM((2, LEVELS, ROWS, COLS), f32),
+            pltpu.VMEM((1, 1), f32),
         ),
         in_specs=[any_space] * 12,
-        out_specs=(any_space, vmem, smem),
+        out_specs=(vmem,) * 3,
         scratch_shapes=[
             pltpu.VMEM((4, LEVELS, ROWS + 16, COLS), f32),
             pltpu.VMEM((4, LEVELS, ROWS + 16, COLS), f32),
@@ -605,10 +661,11 @@
             pltpu.VMEM((2 * COLS, 2 * COLS), jnp.bfloat16),
             pltpu.VMEM((2, per, ROWS, COLS), f32),
             pltpu.VMEM((2, reach - 1, per, ROWS, COLS), f32),
-            pltpu.VMEM((2, 32, 4, COLS), f32),
-            pltpu.VMEM((2, 2, 32, 4, COLS), f32),
+            pltpu.VMEM((2, 2, 2, 16, 4, COLS), f32),
+            pltpu.VMEM((2, 2, 2, 16, 4, COLS), f32),
+            pltpu.VMEM((2, 2, 2, ROWS // 2, COLS), f32),
+            pltpu.VMEM((2, 2, 2, ROWS // 2, COLS), f32),
             pltpu.VMEM((2, ROWS, COLS), f32),
-            pltpu.VMEM((2, 2, ROWS, COLS), f32),
             pltpu.VMEM((2, 32, 16, COLS), f32),
             pltpu.VMEM((2, ROWS, COLS), f32),
             pltpu.VMEM((7, ROWS, COLS), f32),
@@ -618,17 +675,16 @@
             pltpu.VMEM((n_z,) + tile, f32),
             pltpu.SMEM(args[4].shape, jnp.int32),
             pltpu.SMEM(args[5].shape, jnp.int32),
-            pltpu.SMEM(args[6].shape, jnp.int32),
-            pltpu.SMEM(args[7].shape, jnp.int32),
+            pltpu.SMEM((1,), jnp.int32),
+            pltpu.SMEM((1,), jnp.int32),
             pltpu.SMEM(args[8].shape, f32),
             pltpu.VMEM(args[9].shape, jnp.int32),
             pltpu.VMEM(args[10].shape, jnp.int32),
             pltpu.VMEM(args[11].shape, f32),
-            dma((4,)),
+            dma((5,)),
             dma((8,)),
-            dma((2, 2, 2)),
-            dma((2, 2, 2)),
-            dma,
+            dma((2, 2, 2, 2)),
+            dma((2, 2, 2, 2)),
             dma((2,)),
             dma((2, 2, reach)),
             dma((2, reach - 1, 2)),
@@ -640,10 +696,18 @@
             dma((2, n_z - 1)),
         ],
         compiler_params=pltpu.CompilerParams(
-            collective_id=0, has_side_effects=True, vmem_limit_bytes=60 * 1024 * 1024
+            collective_id=0, has_side_effects=True, vmem_limit_bytes=32 * 1024 * 1024
         ),
-    )(*args)
-    return fields, sums[0], sums[1], curv[0, 0]
+    )(*[arg if arg.size == 1 else pltpu.with_memory_space_constraint(arg, pltpu.HBM) for arg in args])
+    sums_shape = jax.ShapeDtypeStruct((LEVELS, ROWS, COLS), f32)
+    fields, grad, hess, curv = pl.pallas_call(
+        deliver,
+        out_shape=(jax.ShapeDtypeStruct(fields.shape, f32), sums_shape, sums_shape, jax.ShapeDtypeStruct((1, 1), f32)),
+        in_specs=[any_space] * 3,
+        out_specs=(hbm,) * 4,
+        scratch_shapes=[dma((4,))],
+    )(*[pltpu.with_memory_space_constraint(value, pltpu.VMEM) for value in (fields, sums, curv)])
+    return fields, grad, hess, curv[0, 0]
 
 
 def solution(mesh):

time: 55.1 us -> 50.4 us (0.915)
  local copies, waits for them, and re-layouts: 2.93 us -> 0 us
  between operations: 3.7 us -> 1.93 us
    squeeze x1 -> x0, local copies, waits for them, and re-layouts: 1.96 us -> none  [local(): return (fields, sums[0], sums[1], curv[0, 0])]
    unnamed x3 -> x0, local copies, waits for them, and re-layouts: 0.97 us -> none
    pallas_call x1 -> x2, Pallas kernels: 48.3 us -> 48.3 us  [the longest x1 46.5 us: local(): pl.pallas_call(functools.partial(kernel, sizes), out_shape=(pltpu.VMEM((1...]
where the time goes in v3:
time: 50.4 us; the launch traced here: 50.2 us
  Pallas kernels  48.3 us (96%)
  between operations  1.93 us (4%)
    pallas_call x1, Pallas kernels, local(): pl.pallas_call(functools.partial(kernel, sizes), out_shape=(pltpu.VMEM((1...  46.5 us
    pallas_call x1, Pallas kernels, local(): pl.pallas_call(deliver, out_shape=(jax.ShapeDtypeStruct(fields.shape, f32...  1.8 us

profile of v3, /device:TPU:1, one launch (start us, length us, event | category | flops | bytes accessed | tf_op | source)
XLA Modules:
  0.0 50.2 jit_solution(5376464849093317892)
XLA Ops:
  1.9 46.5 %shard_map.147 = (f32[1,4,8,64,128]{4,3,2,1,0:T(8,128)S(1)}, f32[2,8,64,128]{3,2,1,0:T(8,128)S(1)}, f32[1,1]{1,0:T(1,128)}) custom-call(f32[1,4,8,64,128]{4,3,2,1,0:T(8,128)} %now_ref.1, f32[1,4,8,64,128]{4,3,2,1,0:T(8,128)} %before_ref.1, f32[8,64,128]{2,1,0:T(8,128)} %speed_ref.1, f32[8,64,128]{2,1,0:T(8,128)} %born_ref.1, s32[512]{0:T(512)} %pml_x_ref.1, ...), custom_call_target="tpu_custom_call" | custom-call | tf_op jit(solution)/shard_map/pallas_call | solution.py:642
  48.4 1.8 %shard_map.148 = (f32[1,4,8,64,128]{4,3,2,1,0:T(8,128)}, f32[8,64,128]{2,1,0:T(8,128)}, f32[8,64,128]{2,1,0:T(8,128)}, f32[1,1]{1,0:T(1,128)}) custom-call(f32[1,4,8,64,128]{4,3,2,1,0:T(8,128)S(1)} %get-tuple-element.11.fields_ref, f32[2,8,64,128]{3,2,1,0:T(8,128)S(1)} %get-tuple-element.12.sums_ref, f32[1,1]{1,0:T(1,128)} %get-tuple-element.13.curv_ref), custom_call_target="tpu_custom_call" | custom-call | tf_op jit(solution)/shard_map/pallas_call | solution.py:703

commit v4 on v3

--- a/solution.py
+++ b/solution.py
@@ -54,7 +54,6 @@
     lap,
     band,
     corner,
-    join,
     direct,
     x_send,
     x_recv,
@@ -84,7 +83,6 @@
     rs_sems,
     ag_sems,
     agsib_sems,
-    last_sems,
     cs_sems,
     cy_sems,
     cx_sems,
@@ -92,7 +90,6 @@
 ):
     shots, n_x, n_y = sizes
     n_z = shots // 2
-    reach = n_z // 2
     per = LEVELS // n_z
     shot = lax.axis_index("shot")
     core = lax.rem(shot, 2)
@@ -102,9 +99,6 @@
 
     def z_id(k):
         return {"shot": lax.rem(z + k + 2 * n_z, n_z) * 2 + core}
-
-    def cross_id(k):
-        return {"shot": lax.rem(z + k + 2 * n_z, n_z) * 2 + 1 - core}
 
     def x_id(k):
         return {"gx": lax.rem(gx + k + n_x, n_x)}
@@ -146,17 +140,16 @@
             ]
         )
     ]
-    for load in loads[:2] + small + loads[2:]:
-        load.start()
-
     barrier = pltpu.get_barrier_semaphore()
     partners = [sib_id]
     partners += [z_id(k) for k in range(1, n_z)]
-    partners += [cross_id(1), cross_id(-1)]
     partners += [x_id(k) for k in range(1, n_x)]
     partners += [y_id(k) for k in range(1, n_y)]
     for who in partners:
         pl.semaphore_signal(barrier, inc=1, device_id=who, device_id_type=MESH)
+
+    for load in loads[:2] + small + loads[2:]:
+        load.start()
 
     whole_x = n_x * ROWS
     whole_y = n_y * COLS
@@ -366,7 +359,7 @@
         if turn == 0:
             packed[pair, block(b), :] = borders(fresh)
 
-    def incident(turn, field):
+    def incident(turn, field, first, last, curv):
         def body(b, curv):
             u = [field[0, lev, inner(b), :] for lev in range(LEVELS)]
             du = [field[1, lev, inner(b), :] for lev in range(LEVELS)]
@@ -398,7 +391,7 @@
             finish(turn, 0, b, fresh)
             return curv
 
-        return lax.fori_loop(0, BLOCKS, body, jnp.zeros((8, COLS), jnp.float32))
+        return lax.fori_loop(first, last, body, curv)
 
     def adjoint(turn, field):
         def body(b, carry):
@@ -459,7 +452,8 @@
         unpack_x(turn, pair)
 
     take(0, 0)
-    incident(0, field0)
+    nothing = jnp.zeros((8, COLS), jnp.float32)
+    incident(0, field0, 0, BLOCKS, nothing)
     pack_x(field1, 1, 0)
     x_copies[1, 0] = send_x(1, 0)
     y_copies[1, 0] = send_y(1, 0)
@@ -472,18 +466,25 @@
     inside(field1, 0)
     inside(field1, 1)
     take(1, 0)
-    curv = incident(1, field1)
-
-    swap = remote(terms.at[1 - core], sib, sib_sems.at[0], sib_sems.at[1], sib_id)
-    swap.start()
+
+    halves = (pl.ds(0, ROWS // 2), pl.ds(ROWS // 2, ROWS // 2))
+    swaps = []
+    curv = nothing
+    for part in range(2):
+        curv = incident(1, field1, part * (BLOCKS // 2), (part + 1) * (BLOCKS // 2), curv)
+        swap = remote(
+            terms.at[1 - core, :, halves[part], :],
+            sib.at[:, halves[part], :],
+            sib_sems.at[0, part],
+            sib_sems.at[1, part],
+            sib_id,
+        )
+        swap.start()
+        swaps.append(swap)
     curv_sib[core] = curv
     curv_swap = remote(curv_sib.at[core], curv_sib.at[core], cs_sems.at[0], cs_sems.at[1], sib_id)
     curv_swap.start()
     take(1, 1)
-    adjoint(1, field1)
-    for copies in list(x_copies.values()) + list(y_copies.values()):
-        for copy in copies:
-            copy.wait_send()
 
     def spread(buffer, place, value, sems, ident, count):
         buffer[place] = value
@@ -506,107 +507,69 @@
     def owner(k):
         return pl.ds(lax.rem(z + k + 2 * n_z, n_z) * per, per)
 
-    halves = (pl.ds(0, ROWS // 2), pl.ds(ROWS // 2, ROWS // 2))
-    full = pl.ds(0, ROWS)
-    signs = (1, -1)
-
-    def add(level, rows, *others):
-        total = terms[core, level, rows, :]
-        for other in others:
-            total = total + other
-        terms[core, level, rows, :] = total
-
-    def share(way, k):
-        copy = remote(
-            terms.at[core, owner(signs[way] * k), full, :],
-            direct.at[way, k - 1],
-            rs_sems.at[0, way, k],
-            rs_sems.at[1, way, k],
-            z_id(signs[way] * k),
-        )
-        copy.start()
-        return copy
-
-    swap.wait()
-    joins = []
-    for way in range(2):
-        level = owner(reach)
-        rows = halves[way]
-        add(level, rows, sib[level, rows, :])
-        copy = remote(
-            terms.at[core, level, rows, :],
-            join.at[way, :, rows, :],
-            rs_sems.at[0, way, 0],
-            rs_sems.at[1, way, 0],
-            z_id(signs[way]),
-        )
-        copy.start()
-        joins.append(copy)
-    shares = []
-    for k in range(reach - 2, 0, -1):
-        for way in range(2):
-            level = owner(signs[way] * k)
-            add(level, full, sib[level, full, :])
-            shares.append(share(way, k))
-    curv_swap.wait()
-    curv = curv_sib[0] + curv_sib[1]
-    sent_y = spread(curv_x, gx, curv, cx_sems, x_id, n_x)
-    for way in range(2):
-        level = owner(signs[way] * (reach - 1))
-        add(level, full, sib[level, full, :])
-    add(owner(0), full, sib[owner(0), full, :])
-    for way in range(2):
-        joins[way].wait_recv()
-        level = owner(signs[way] * (reach - 1))
-        add(level, halves[way], join[way, :, halves[way], :])
-        shares.append(share(way, reach - 1))
-    curv = gather(sent_y, curv_x, n_x)
-    sent_x = spread(curv_y, gy, curv, cy_sems, y_id, n_y)
-    for copy in shares:
-        copy.wait_recv()
-    total = terms[core, owner(0)]
-    for way in range(2):
-        for k in range(1, reach):
-            total = total + direct[way, k - 1]
-    sums_ref[core, owner(0)] = total * (1.0 / shots)
-
-    def pass_on(level, rows, pair, who):
+    order = sorted(range(1, n_z), key=lambda k: -min(k, n_z - k))
+    shares = {}
+    for part in range(2):
+        rows = halves[part]
+        swaps[part].wait_recv()
+        for k in order:
+            level = owner(k)
+            terms[core, level, rows, :] = terms[core, level, rows, :] + sib[level, rows, :]
+            shares[part, k] = remote(
+                terms.at[core, level, rows, :],
+                direct.at[part, k - 1],
+                rs_sems.at[0, part, k - 1],
+                rs_sems.at[1, part, k - 1],
+                z_id(k),
+            )
+            shares[part, k].start()
+        if part == 0:
+            curv_swap.wait()
+            curv = curv_sib[0] + curv_sib[1]
+            sent_y = spread(curv_x, gx, curv, cx_sems, x_id, n_x)
+    adjoint(1, field1)
+
+    def pass_on(level, rows, sems, part, k, who):
         copy = remote(
             sums_ref.at[core, level, rows, :],
             sums_ref.at[core, level, rows, :],
-            pair.at[0],
-            pair.at[1],
+            sems.at[0, part, k],
+            sems.at[1, part, k],
             who,
         )
         copy.start()
         return copy
 
     spreads = {}
-    for k in range(reach - 1, 0, -1):
-        for way in range(2):
-            spreads[way, k] = pass_on(
-                owner(0), full, ag_sems.at[way, k - 1], z_id(signs[way] * k)
-            )
-    across = [pass_on(owner(0), full, agsib_sems.at[0], sib_id)]
-    for copy in joins + shares:
-        copy.wait_send()
+    across = []
+    for part in range(2):
+        rows = halves[part]
+        total = terms[core, owner(0), rows, :] + sib[owner(0), rows, :]
+        for k in reversed(order):
+            shares[part, k].wait_recv()
+            total = total + direct[part, k - 1]
+        sums_ref[core, owner(0), rows, :] = total * (1.0 / shots)
+        for k in order:
+            spreads[part, k] = pass_on(owner(0), rows, ag_sems, part, k - 1, z_id(k))
+        across.append(pass_on(owner(0), rows, agsib_sems, part, 0, sib_id))
+        if part == 0:
+            curv = gather(sent_y, curv_x, n_x)
+            sent_x = spread(curv_y, gy, curv, cy_sems, y_id, n_y)
     curv = gather(sent_x, curv_y, n_y)
     sent_z = spread(curv_z, z, curv, cz_sems, z_id, n_z)
-    lasts = []
-    for k in range(1, reach):
-        for way in range(2):
-            spreads[way, k].wait_recv()
-            level = owner(-signs[way] * k)
-            if k == reach - 1:
-                lasts.append(pass_on(level, halves[way], last_sems.at[way, 0], z_id(signs[way])))
-                lasts.append(pass_on(level, halves[way], last_sems.at[way, 1], cross_id(signs[way])))
-            across.append(pass_on(level, full, agsib_sems.at[2 * k - 1 + way], sib_id))
+    for part in range(2):
+        for k in reversed(order):
+            spreads[part, k].wait_recv()
+            across.append(pass_on(owner(-k), halves[part], agsib_sems, part, k, sib_id))
     curv = gather(sent_z, curv_z, n_z)
     cells = LEVELS * whole_x * whole_y
     curv_ref[...] = jnp.sum(curv, keepdims=True) * (1.0 / (shots * math.sqrt(cells)))
-    for copy in spreads.values():
+    for copies in list(x_copies.values()) + list(y_copies.values()):
+        for copy in copies:
+            copy.wait_send()
+    for copy in swaps + list(shares.values()) + list(spreads.values()):
         copy.wait_send()
-    for copy in across + lasts:
+    for copy in across:
         copy.wait()
 
 
@@ -631,7 +594,6 @@
 def local(sizes, *args):
     shots, n_x, n_y = sizes
     n_z = shots // 2
-    reach = n_z // 2
     per = LEVELS // n_z
     any_space = pl.BlockSpec(memory_space=pl.ANY)
     hbm = pl.BlockSpec(memory_space=pltpu.HBM)
@@ -659,8 +621,7 @@
             pltpu.VMEM((4, LEVELS, ROWS, COLS), f32),
             pltpu.VMEM((2 * COLS, 2 * COLS), jnp.bfloat16),
             pltpu.VMEM((2 * COLS, 2 * COLS), jnp.bfloat16),
-            pltpu.VMEM((2, per, ROWS, COLS), f32),
-            pltpu.VMEM((2, reach - 1, per, ROWS, COLS), f32),
+            pltpu.VMEM((2, n_z - 1, per, ROWS // 2, COLS), f32),
             pltpu.VMEM((2, 2, 2, 16, 4, COLS), f32),
             pltpu.VMEM((2, 2, 2, 16, 4, COLS), f32),
             pltpu.VMEM((2, 2, 2, ROWS // 2, COLS), f32),
@@ -685,11 +646,10 @@
             dma((8,)),
             dma((2, 2, 2, 2)),
             dma((2, 2, 2, 2)),
-            dma((2,)),
-            dma((2, 2, reach)),
-            dma((2, reach - 1, 2)),
-            dma((2 * reach - 1, 2)),
-            dma((2, 2, 2)),
+            dma((2, 2)),
+            dma((2, 2, n_z - 1)),
+            dma((2, 2, n_z - 1)),
+            dma((2, 2, n_z)),
             dma((2,)),
             dma((2, n_y - 1)),
             dma((2, n_x - 1)),

time: 50.4 us -> 48.6 us (0.964)
  Pallas kernels: 48.3 us -> 46.5 us
    pallas_call x1, Pallas kernels: 46.5 us -> 44.7 us  [local(): pl.pallas_call(functools.partial(kernel, sizes), out_shape=(pltpu.VMEM((1...]
where the time goes in v4:
time: 48.6 us; the launch traced here: 48.4 us
  Pallas kernels  46.5 us (96%)
  between operations  1.93 us (4%)
    pallas_call x1, Pallas kernels, local(): pl.pallas_call(functools.partial(kernel, sizes), out_shape=(pltpu.VMEM((1...  44.7 us
    pallas_call x1, Pallas kernels, local(): pl.pallas_call(deliver, out_shape=(jax.ShapeDtypeStruct(fields.shape, f32...  1.8 us

profile of v4, /device:TPU:1, one launch (start us, length us, event | category | flops | bytes accessed | tf_op | source)
XLA Modules:
  0.0 48.4 jit_solution(5609033803051616558)
XLA Ops:
  1.9 44.7 %shard_map.147 = (f32[1,4,8,64,128]{4,3,2,1,0:T(8,128)S(1)}, f32[2,8,64,128]{3,2,1,0:T(8,128)S(1)}, f32[1,1]{1,0:T(1,128)}) custom-call(f32[1,4,8,64,128]{4,3,2,1,0:T(8,128)} %now_ref.1, f32[1,4,8,64,128]{4,3,2,1,0:T(8,128)} %before_ref.1, f32[8,64,128]{2,1,0:T(8,128)} %speed_ref.1, f32[8,64,128]{2,1,0:T(8,128)} %born_ref.1, s32[512]{0:T(512)} %pml_x_ref.1, ...), custom_call_target="tpu_custom_call" | custom-call | tf_op jit(solution)/shard_map/pallas_call | solution.py:604
  46.6 1.8 %shard_map.148 = (f32[1,4,8,64,128]{4,3,2,1,0:T(8,128)}, f32[8,64,128]{2,1,0:T(8,128)}, f32[8,64,128]{2,1,0:T(8,128)}, f32[1,1]{1,0:T(1,128)}) custom-call(f32[1,4,8,64,128]{4,3,2,1,0:T(8,128)S(1)} %get-tuple-element.11.fields_ref, f32[2,8,64,128]{3,2,1,0:T(8,128)S(1)} %get-tuple-element.12.sums_ref, f32[1,1]{1,0:T(1,128)} %get-tuple-element.13.curv_ref), custom_call_target="tpu_custom_call" | custom-call | tf_op jit(solution)/shard_map/pallas_call | solution.py:663

commit v5 on v4

--- a/solution.py
+++ b/solution.py
@@ -87,6 +87,7 @@
     cy_sems,
     cx_sems,
     cz_sems,
+    relay,
 ):
     shots, n_x, n_y = sizes
     n_z = shots // 2
@@ -141,12 +142,17 @@
         )
     ]
     barrier = pltpu.get_barrier_semaphore()
-    partners = [sib_id]
-    partners += [z_id(k) for k in range(1, n_z)]
-    partners += [x_id(k) for k in range(1, n_x)]
-    partners += [y_id(k) for k in range(1, n_y)]
+    neighbours = [z_id(1), z_id(-1), x_id(1), x_id(-1), y_id(1), y_id(-1)]
+    partners = [sib_id] + neighbours
     for who in partners:
         pl.semaphore_signal(barrier, inc=1, device_id=who, device_id_type=MESH)
+
+    def tell(turn):
+        for who in neighbours:
+            pl.semaphore_signal(relay.at[turn], inc=1, device_id=who, device_id_type=MESH)
+
+    def hear(turn):
+        pl.semaphore_wait(relay.at[turn], len(neighbours))
 
     for load in loads[:2] + small + loads[2:]:
         load.start()
@@ -436,10 +442,13 @@
         x_copies[0, pair] = send_x(0, pair)
         pack_y(field0, pair)
         y_copies[0, pair] = send_y(0, pair)
+    tell(0)
     build_weights()
     build_planes()
     inside(field0, 0)
     inside(field0, 1)
+    hear(0)
+    tell(1)
     for load in loads[2:]:
         load.wait()
 
@@ -463,6 +472,8 @@
     x_copies[1, 1] = send_x(1, 1)
     y_copies[1, 1] = send_y(1, 1)
 
+    hear(1)
+    tell(2)
     inside(field1, 0)
     inside(field1, 1)
     take(1, 0)
@@ -485,6 +496,7 @@
     curv_swap = remote(curv_sib.at[core], curv_sib.at[core], cs_sems.at[0], cs_sems.at[1], sib_id)
     curv_swap.start()
     take(1, 1)
+    hear(2)
 
     def spread(buffer, place, value, sems, ident, count):
         buffer[place] = value
@@ -654,6 +666,7 @@
             dma((2, n_y - 1)),
             dma((2, n_x - 1)),
             dma((2, n_z - 1)),
+            pltpu.SemaphoreType.REGULAR((3,)),
         ],
         compiler_params=pltpu.CompilerParams(
             collective_id=0, has_side_effects=True, vmem_limit_bytes=32 * 1024 * 1024

time: 48.6 us -> 46.2 us (0.951)
  Pallas kernels: 46.5 us -> 44.1 us
    pallas_call x1, Pallas kernels: 44.7 us -> 42.3 us  [local(): pl.pallas_call(functools.partial(kernel, sizes), out_shape=(pltpu.VMEM((1...]
where the time goes in v5:
time: 46.2 us; the launch traced here: 46 us
  Pallas kernels  44.1 us (95%)
  between operations  1.93 us (4%)
    pallas_call x1, Pallas kernels, local(): pl.pallas_call(functools.partial(kernel, sizes), out_shape=(pltpu.VMEM((1...  42.3 us
    pallas_call x1, Pallas kernels, local(): pl.pallas_call(deliver, out_shape=(jax.ShapeDtypeStruct(fields.shape, f32...  1.8 us

profile of v5, /device:TPU:1, one launch (start us, length us, event | category | flops | bytes accessed | tf_op | source)
XLA Modules:
  0.0 46.0 jit_solution(16036273480472783183)
XLA Ops:
  1.9 42.3 %shard_map.147 = (f32[1,4,8,64,128]{4,3,2,1,0:T(8,128)S(1)}, f32[2,8,64,128]{3,2,1,0:T(8,128)S(1)}, f32[1,1]{1,0:T(1,128)}) custom-call(f32[1,4,8,64,128]{4,3,2,1,0:T(8,128)} %now_ref.1, f32[1,4,8,64,128]{4,3,2,1,0:T(8,128)} %before_ref.1, f32[8,64,128]{2,1,0:T(8,128)} %speed_ref.1, f32[8,64,128]{2,1,0:T(8,128)} %born_ref.1, s32[512]{0:T(512)} %pml_x_ref.1, ...), custom_call_target="tpu_custom_call" | custom-call | tf_op jit(solution)/shard_map/pallas_call | solution.py:616
  44.2 1.8 %shard_map.148 = (f32[1,4,8,64,128]{4,3,2,1,0:T(8,128)}, f32[8,64,128]{2,1,0:T(8,128)}, f32[8,64,128]{2,1,0:T(8,128)}, f32[1,1]{1,0:T(1,128)}) custom-call(f32[1,4,8,64,128]{4,3,2,1,0:T(8,128)S(1)} %get-tuple-element.11.fields_ref, f32[2,8,64,128]{3,2,1,0:T(8,128)S(1)} %get-tuple-element.12.sums_ref, f32[1,1]{1,0:T(1,128)} %get-tuple-element.13.curv_ref), custom_call_target="tpu_custom_call" | custom-call | tf_op jit(solution)/shard_map/pallas_call | solution.py:676

commit v6 on v5

--- a/solution.py
+++ b/solution.py
@@ -475,7 +475,6 @@
     hear(1)
     tell(2)
     inside(field1, 0)
-    inside(field1, 1)
     take(1, 0)
 
     halves = (pl.ds(0, ROWS // 2), pl.ds(ROWS // 2, ROWS // 2))
@@ -495,7 +494,6 @@
     curv_sib[core] = curv
     curv_swap = remote(curv_sib.at[core], curv_sib.at[core], cs_sems.at[0], cs_sems.at[1], sib_id)
     curv_swap.start()
-    take(1, 1)
     hear(2)
 
     def spread(buffer, place, value, sems, ident, count):
@@ -539,6 +537,8 @@
             curv_swap.wait()
             curv = curv_sib[0] + curv_sib[1]
             sent_y = spread(curv_x, gx, curv, cx_sems, x_id, n_x)
+    inside(field1, 1)
+    take(1, 1)
     adjoint(1, field1)
 
     def pass_on(level, rows, sems, part, k, who):

time: 46.2 us -> 45.6 us (0.987)
  Pallas kernels: 44.1 us -> 43.5 us
    pallas_call x1, Pallas kernels: 42.3 us -> 41.7 us  [local(): pl.pallas_call(functools.partial(kernel, sizes), out_shape=(pltpu.VMEM((1...]
where the time goes in v6:
time: 45.6 us; the launch traced here: 45.4 us
  Pallas kernels  43.5 us (95%)
  between operations  1.93 us (4%)
    pallas_call x1, Pallas kernels, local(): pl.pallas_call(functools.partial(kernel, sizes), out_shape=(pltpu.VMEM((1...  41.7 us
    pallas_call x1, Pallas kernels, local(): pl.pallas_call(deliver, out_shape=(jax.ShapeDtypeStruct(fields.shape, f32...  1.8 us

profile of v6, /device:TPU:1, one launch (start us, length us, event | category | flops | bytes accessed | tf_op | source)
XLA Modules:
  0.0 45.4 jit_solution(2388203972309141019)
XLA Ops:
  1.9 41.7 %shard_map.147 = (f32[1,4,8,64,128]{4,3,2,1,0:T(8,128)S(1)}, f32[2,8,64,128]{3,2,1,0:T(8,128)S(1)}, f32[1,1]{1,0:T(1,128)}) custom-call(f32[1,4,8,64,128]{4,3,2,1,0:T(8,128)} %now_ref.1, f32[1,4,8,64,128]{4,3,2,1,0:T(8,128)} %before_ref.1, f32[8,64,128]{2,1,0:T(8,128)} %speed_ref.1, f32[8,64,128]{2,1,0:T(8,128)} %born_ref.1, s32[512]{0:T(512)} %pml_x_ref.1, ...), custom_call_target="tpu_custom_call" | custom-call | tf_op jit(solution)/shard_map/pallas_call | solution.py:616
  43.6 1.8 %shard_map.148 = (f32[1,4,8,64,128]{4,3,2,1,0:T(8,128)}, f32[8,64,128]{2,1,0:T(8,128)}, f32[8,64,128]{2,1,0:T(8,128)}, f32[1,1]{1,0:T(1,128)}) custom-call(f32[1,4,8,64,128]{4,3,2,1,0:T(8,128)S(1)} %get-tuple-element.11.fields_ref, f32[2,8,64,128]{3,2,1,0:T(8,128)S(1)} %get-tuple-element.12.sums_ref, f32[1,1]{1,0:T(1,128)} %get-tuple-element.13.curv_ref), custom_call_target="tpu_custom_call" | custom-call | tf_op jit(solution)/shard_map/pallas_call | solution.py:676
